TPU v7x, 32 devices: a whole 2x2x4 slice. The times are simulated.
32 devices in a mesh: row: 4 (over y, x), lat: 8 (over z, core).
Axes of the slice: x: 2, y: 2, z: 4, core: 2. Of those that a mesh axis runs over, the one named last changes fastest.
Arguments:
- tokens: bfloat16 [4, 2048, 512], P('row', 'lat'), may hold values from -6 to 6
- latents: bfloat16 [4, 8192, 512], P('row', 'lat'), may hold values from -6 to 6
- segment_ids: int32 [4, 2048], P('row', 'lat'), may hold values from 0 to 3, as said below
- pad_mask: int32 [4, 2048], P('row', 'lat'), may hold values from 0 to 1, as said below
- block_scene: int32 [4, 4], P('row'), may hold values from 0 to 3, each once within a row
- out_grad: bfloat16 [4, 8192, 512], P('row', 'lat'), may hold values from -6 to 6
- gain_cross_q: bfloat16 [512], P('lat'), may hold values from 0.099609375 to 1.8984375
- gain_cross_kv: bfloat16 [512], P('lat'), may hold values from 0.099609375 to 1.8984375
- w_cross_q: bfloat16 [512, 512], P('lat'), may hold values from -0.5 to 0.5
- w_cross_kv: bfloat16 [512, 1024], P('lat'), may hold values from -0.25 to 0.25
- w_cross_out: bfloat16 [512, 512], P('lat'), may hold values from -1.5 to 1.5
- gain_mlp1: bfloat16 [512], P('lat'), may hold values from 0.099609375 to 1.8984375
- w_up1: bfloat16 [512, 2048], P('lat'), may hold values from -0.25 to 0.25
- w_down1: bfloat16 [2048, 512], P('lat'), may hold values from -0.1875 to 0.1875
- gain_self: bfloat16 [512], P('lat'), may hold values from 0.099609375 to 1.8984375
- w_self_qkv: bfloat16 [512, 1536], P('lat'), may hold values from -0.375 to 0.375
- w_self_out: bfloat16 [512, 512], P('lat'), may hold values from -1 to 1
- gain_mlp2: bfloat16 [512], P('lat'), may hold values from 0.099609375 to 1.8984375
- w_up2: bfloat16 [512, 2048], P('lat'), may hold values from -0.25 to 0.25
- w_down2: bfloat16 [2048, 512], P('lat'), may hold values from -0.1875 to 0.1875
Outputs:
- out: float32 [4, 8192, 512], P('row', 'lat')
- latent_grad: float32 [4, 8192, 512], P('row', 'lat')
- token_grad: float32 [4, 2048, 512], P('row', 'lat')
- grad_gain_cross_q: float32 [512], P('lat')
- grad_gain_cross_kv: float32 [512], P('lat')
- grad_w_cross_q: float32 [512, 512], P('lat')
- grad_w_cross_kv: float32 [512, 1024], P('lat')
- grad_w_cross_out: float32 [512, 512], P('lat')
- grad_gain_mlp1: float32 [512], P('lat')
- grad_w_up1: float32 [512, 2048], P('lat')
- grad_w_down1: float32 [2048, 512], P('lat')
- grad_gain_self: float32 [512], P('lat')
- grad_w_self_qkv: float32 [512, 1536], P('lat')
- grad_w_self_out: float32 [512, 512], P('lat')
- grad_gain_mlp2: float32 [512], P('lat')
- grad_w_up2: float32 [512, 2048], P('lat')
- grad_w_down2: float32 [2048, 512], P('lat')
Inputs may be any that keep to these rules, and one draw needn't show every extreme that they name: `segment_ids`: each row packs scenes 0 to 3 in order, each in consecutive slots; a scene holds between 256 and 480 slots, and scene 0 exactly the latter; slots after the last scene are padding and carry any scene number. `pad_mask`: 1 exactly on the slots of the scenes, 0 on the padding after them. In each row a permutation of the scenes: latent block b belongs to scene block_scene[row, b].
All inputs are finite; a program needn't handle non-finite values.
Results may differ from a plain program's by a relative error of at most 0.028.
Values may be sent and summed in bfloat16 or wider, within the bound.
A program may use at most 384 MiB of HBM per device.

v0:
```python
import functools

import jax
import jax.numpy as jnp
from jax import lax
from jax.experimental import pallas as pl
from jax.experimental.pallas import tpu as pltpu
from jax.sharding import PartitionSpec as P

D = 512
FF = 2048
HEADS = 8
LAT_SCENE = 2048
HEAD = D // HEADS
PAIRS = HEADS // 2
LANES = 128
FF_STEP = 512
EPS = 1e-05
NEG = -1e30
CROSS_SCALE = D ** (-0.5)
SELF_SCALE = HEAD ** (-0.5)
GELU_C = 0.7978845608028654
GELU_K = 0.044715
VMEM_LIMIT = 60 * 1024 * 1024
F32 = jnp.float32
BF16 = jnp.bfloat16


def low(value):
    return value.astype(BF16)


def dot(left, right):
    return jnp.dot(left, right, preferred_element_type=F32)


def dot_nt(left, right):
    return lax.dot_general(left, right, (((1,), (1,)), ((), ())), preferred_element_type=F32)


def dot_tn(left, right):
    return lax.dot_general(left, right, (((0,), (0,)), ((), ())), preferred_element_type=F32)


def normed(value):
    centered = value - jnp.mean(value, axis=-1, keepdims=True)
    factor = lax.rsqrt(jnp.mean(centered * centered, axis=-1, keepdims=True) + EPS)
    return centered * factor, factor


def norm_back(grad, unit, factor, gain):
    scaled = grad * gain
    inner = (
        scaled
        - jnp.mean(scaled, axis=-1, keepdims=True)
        - unit * jnp.mean(scaled * unit, axis=-1, keepdims=True)
    )
    return factor * inner, jnp.sum(grad * unit, axis=0, keepdims=True)


def gelu(u):
    return 0.5 * u * (1.0 + jnp.tanh(GELU_C * (u + GELU_K * u * u * u)))


def gelu_both(u):
    square = u * u
    t = jnp.tanh(GELU_C * u * (1.0 + GELU_K * square))
    half = 0.5 * (1.0 + t)
    slope = half + 0.5 * u * (1.0 - t * t) * (GELU_C * (1.0 + 3.0 * GELU_K * square))
    return u * half, slope


def call(kernel, grid, ins, outs, scratch=(), comm=None, collective_id=None):
    in_specs = [ANYWHERE if block is None else pl.BlockSpec(block, index) for _, block, index in ins]
    out_specs = [ANYWHERE if block is None else pl.BlockSpec(block, index) for _, _, block, index in outs]
    out_shape = [jax.ShapeDtypeStruct(shape, kind) for shape, kind, _, _ in outs]
    arrays, scratch = [array for array, _, _ in ins], list(scratch)
    if comm is not None:
        arrays += comm.inputs
        in_specs += comm.in_specs
        out_shape += comm.out_shapes
        out_specs += comm.out_specs
        scratch += comm.scratch
    return pl.pallas_call(
        kernel,
        grid=grid,
        in_specs=in_specs,
        out_specs=out_specs,
        out_shape=out_shape,
        scratch_shapes=scratch,
        compiler_params=pltpu.CompilerParams(
            vmem_limit_bytes=VMEM_LIMIT,
            collective_id=None if comm is None else collective_id,
            has_side_effects=comm is not None,
        ),
    )(*arrays)


def inside(shape):
    return pl.BlockSpec(shape, lambda *_: (0,) * len(shape))


ANYWHERE = pl.BlockSpec(memory_space=pl.ANY)


def flat(*_):
    return (0, 0)


def column(c):
    return lambda *_: (0, c)


def rows_of(i, *_):
    return (i, 0)


def front_kernel(
    lat_ref, tok_ref, tags_ref, scene_ref, gain_ref, wq_ref, wkv_ref, wout_ref, wup_ref, wdown_ref, wqkv_ref,
    x1_ref, x2_ref, q_ref, p_ref, o_ref, kv_ref, q2_ref, k2_ref, v2_ref, win_ref, start_ref,
    bias_ref, sem,
):
    @pl.when(pl.program_id(0) == 0)
    def _():
        span, slots = win_ref.shape[0], tok_ref.shape[0]
        tags, scene = tags_ref[...].astype(F32), scene_ref[0, 0].astype(F32)
        count = lambda chosen: jnp.sum(jnp.where(chosen, 1.0, 0.0)).astype(jnp.int32)
        before = count((tags >= 0.0) & (tags < scene))
        length = count(tags == scene)
        start = pl.multiple_of(jnp.minimum(before // 16 * 16, slots - span), 16)
        copy = pltpu.make_async_copy(tok_ref.at[pl.ds(start, span)], win_ref, sem)
        copy.start()
        start_ref[...] = jnp.full(start_ref.shape, start, jnp.int32)
        slot = lax.broadcasted_iota(jnp.int32, bias_ref.shape, 1) + start
        bias_ref[...] = jnp.where((slot >= before) & (slot < before + length), 0.0, NEG)
        copy.wait()
        unit, _ = normed(win_ref[...].astype(F32))
        kv_ref[...] = low(dot(low(unit * gain_ref[1:2, :]), wkv_ref[...]))

    x = lat_ref[...].astype(F32)
    unit, _ = normed(x)
    q = low(dot(low(unit * gain_ref[0:1, :]), wq_ref[...]))
    q_ref[...] = q
    s = dot_nt(q, kv_ref[:, :D]) * CROSS_SCALE + bias_ref[0:1, :]
    e = jnp.exp(s - jnp.max(s, axis=1, keepdims=True))
    p = low(e / jnp.sum(e, axis=1, keepdims=True))
    p_ref[...] = p
    o = low(dot(p, kv_ref[:, D:]))
    o_ref[...] = o
    x1 = x + dot(o, wout_ref[...])
    x1_ref[...] = x1
    unit, _ = normed(x1)
    m1 = low(unit * gain_ref[2:3, :])
    total = x1
    for c in range(FF // FF_STEP):
        cols = slice(c * FF_STEP, (c + 1) * FF_STEP)
        h = low(gelu(dot(m1, wup_ref[:, cols])))
        total = total + dot(h, wdown_ref[cols, :])
    x2_ref[...] = total
    unit, _ = normed(total)
    bn = low(unit * gain_ref[3:4, :])
    q2_ref[...] = low(dot(bn, wqkv_ref[:, :D])) * SELF_SCALE
    k2_ref[...] = low(dot(bn, wqkv_ref[:, D : 2 * D]))
    v2_ref[...] = low(dot(bn, wqkv_ref[:, 2 * D :]))


def front(latents, tokens, tags, scene, span, gains, mix, up1, down1, qkv):
    rows = latents.shape[0]
    block = min(rows, 512)
    r = (block, D)
    return call(
        front_kernel,
        (rows // block,),
        [
            (latents, r, rows_of),
            (tokens, None, None),
            (tags, tags.shape, flat),
            (scene, scene.shape, flat),
            (gains, (8, D), flat),
            (mix, (D, D), column(2)),
            (mix, (D, 2 * D), column(0)),
            (mix, (D, D), column(3)),
            (up1, (D, FF), flat),
            (down1, (FF, D), flat),
            (qkv, (D, 3 * D), flat),
        ],
        [
            ((rows, D), F32, r, rows_of),
            ((rows, D), F32, r, rows_of),
            ((rows, D), BF16, r, rows_of),
            ((rows, span), BF16, (block, span), rows_of),
            ((rows, D), BF16, r, rows_of),
            ((span, 2 * D), BF16, (span, 2 * D), flat),
            ((rows, D), BF16, r, rows_of),
            ((rows, D), BF16, r, rows_of),
            ((rows, D), BF16, r, rows_of),
            ((span, D), BF16, (span, D), flat),
            ((8, LANES), jnp.int32, (8, LANES), flat),
        ],
        [pltpu.VMEM((8, span), F32), pltpu.SemaphoreType.DMA],
    )


def lane_is(shape, head):
    lane = lax.broadcasted_iota(jnp.int32, shape, 1)
    return (lane < HEAD) if head == 0 else (lane >= HEAD)


def only(value, head):
    return jnp.where(lane_is(value.shape, head), value, jnp.zeros_like(value))


def self_forward_kernel(parts, steps, comm, q_ref, *refs):
    refs = list(refs)
    take = lambda n: [refs.pop(0) for _ in range(n)]
    pair, step = pl.program_id(0), pl.program_id(1)
    point = pair * steps + step
    if comm is None:
        k_refs, v_refs = take(parts), take(parts)
        o_ref, p_ref, scale_ref = take(3)
        ones_refs = refs
    else:
        (k_ref,), (v_ref,) = take(1), take(1)
        both = take(2)
        ins = take(len(comm.inputs))
        o_ref, p_ref, scale_ref, k_more, v_more = take(5)
        outs = take(len(comm.out_shapes))
        ones_refs, (landed,), sems = take(2), take(1), take(2)
        comm.bind(ins, outs, refs)
        k_refs, v_refs = (k_ref, k_more), (v_ref, v_more)

        def to_core(i, p):
            cols = pl.ds(p * LANES, LANES)
            return send(both[i].at[:, cols], landed.at[i, p], sems, (i, p), comm.here.to_core)

        @pl.when(point == 0)
        def _():
            comm.here.greet()
            for p in range(PAIRS):
                for i in range(2):
                    to_core(i, p).start()
            comm.begin()

        pl.when(point == 1)(comm.begin_sends)
        for i in range(comm.steps):
            pl.when(point == SHIFT + i)(functools.partial(comm.step, i))

        @pl.when(step == 0)
        def _():
            for i, ref in enumerate((k_more, v_more)):
                arrived = landed.at[i, pair]
                send(arrived, arrived, sems, (i, pair), comm.here.to_core).wait_recv()
                ref[...] = arrived[...]

    @pl.when(step == 0)
    def _():
        for v_ref, ones_ref in zip(v_refs, ones_refs):
            v = v_ref[...]
            for head in range(2):
                ones_ref[head] = jnp.where(lane_is(v.shape, head), v, jnp.ones_like(v))

    q = q_ref[...]
    outs, scales = [], []
    for head in range(2):
        scores = [dot_nt(only(q, head), k_ref[...]) for k_ref in k_refs]
        top = functools.reduce(jnp.maximum, [jnp.max(s, axis=1, keepdims=True) for s in scores])
        mixed, first = None, 0
        for s, ones_ref in zip(scores, ones_refs):
            p = low(jnp.exp(s - top))
            p_ref[head, :, first : first + p.shape[1]] = p
            first += p.shape[1]
            term = dot(p, ones_ref[head])
            mixed = term if mixed is None else mixed + term
        scales.append(1.0 / pltpu.roll(mixed, HEAD, 1))
        outs.append(mixed * scales[-1])
    left = lane_is(outs[0].shape, 0)
    o_ref[...] = low(jnp.where(left, outs[0], outs[1]))
    scale_ref[...] = jnp.where(left, scales[0], scales[1])

    if comm is not None:
        @pl.when(point == PAIRS * steps - 1)
        def _():
            for p in range(PAIRS):
                for i in range(2):
                    to_core(i, p).wait_send()
            comm.finish()


def self_forward(q2, keys, values, comm=None):
    rows = q2.shape[0]
    block = min(rows, 256)
    parts = len(keys)
    total = sum(k.shape[0] for k in keys) * (1 if comm is None else 2)
    whole = lambda array: (array, (array.shape[0], LANES), lambda p, i: (0, p))
    more = ((rows, D), BF16, (rows, LANES), lambda p, i: (0, p))
    beside = comm is not None
    return call(
        functools.partial(self_forward_kernel, parts, rows // block, comm),
        (PAIRS, rows // block),
        [(q2, (block, LANES), lambda p, i: (i, p))]
        + [whole(k) for k in keys]
        + [whole(v) for v in values]
        + ([(keys[0], None, None), (values[0], None, None)] if beside else []),
        [
            ((rows, D), BF16, (block, LANES), lambda p, i: (i, p)),
            ((HEADS, rows, total), BF16, (2, block, total), lambda p, i: (p, i, 0)),
            ((rows, D), F32, (block, LANES), lambda p, i: (i, p)),
        ]
        + ([more, more] if beside else []),
        [pltpu.VMEM((2, k.shape[0], LANES), BF16) for k in keys * (2 if beside else 1)]
        + ([pltpu.VMEM((2, PAIRS, rows, LANES), BF16)] + sem_pair(2, PAIRS) if beside else []),
        comm=comm,
        collective_id=3,
    )


def run_beside(comm, point, plan, odd):
    for when, work in plan.items():
        if when % 2 != odd:
            continue
        def run(when=when, work=work):
            if when == 0:
                comm.here.greet()
            for name, k in work:
                getattr(comm, name)(k)
        pl.when(point == when)(run)


SELF_PLAN = {
    0: (("start", 0), ("start", 1), ("start", 2)),
    4: (("in_chip", 0),),
    6: (("in_chip", 1),),
    7: (("in_chip", 2),),
    10: (("in_pairs", 0),),
    15: (("in_pairs", 1),),
    16: (("in_pairs", 2),),
    18: (("in_plane", 0),),
    20: (("in_plane", 1), ("turn0", 0)),
    21: (("in_plane", 2),),
    22: (("turn1", 0), ("turn0", 1)),
    24: (("turn2", 0), ("turn1", 1), ("turn0", 2)),
    26: (("in_line", 0), ("turn2", 1), ("turn1", 2)),
    28: (("in_line", 1), ("turn2", 2)),
    30: (("in_line", 2),),
    31: (("end", 0), ("end", 1), ("end", 2)),
}


def self_backward_kernel(parts, steps, comm, q_ref, do_ref, o_ref, scale_ref, p_ref, *refs):
    refs = list(refs)
    take = lambda n: [refs.pop(0) for _ in range(n)]
    pair, step = pl.program_id(0), pl.program_id(1)
    point = 2 * (pair * steps + step)
    k_refs, v_refs = take(parts), take(parts)
    if comm is None:
        (dq_ref,), dk_refs, dv_refs = take(1), take(parts), take(parts)
        dk_sums, dv_sums = take(parts), take(parts)
    else:
        ins = take(len(comm.inputs))
        dq_ref, dk_ref, dv_ref, *landed = take(5)
        outs = take(len(comm.out_shapes))
        dk_sums, dv_sums, (stage,), sems = take(parts), take(parts), take(1), take(2)
        comm.bind(ins, outs, refs)
        dk_refs, dv_refs = (dk_ref, stage.at[0, pair]), (dv_ref, stage.at[1, pair])

        def to_core(i, p):
            cols = pl.ds(pl.multiple_of(p * LANES, LANES), LANES)
            return send(stage.at[i, p], landed[i].at[:, cols], sems, (i, p), comm.here.to_core)

        run_beside(comm, point, SELF_PLAN, 0)

    @pl.when(step == 0)
    def _():
        for ref in (*dk_sums, *dv_sums):
            ref[...] = jnp.zeros_like(ref)

    q = q_ref[...]
    do = low(do_ref[...].astype(F32) * scale_ref[...])
    product = do.astype(F32) * o_ref[...].astype(F32)
    q_turned, do_turned = jnp.transpose(q), jnp.transpose(do)
    dqs = []
    for head in range(2):
        rows = slice(head * HEAD, (head + 1) * HEAD)
        doz = only(do, head)
        delta = jnp.sum(only(product, head), axis=1, keepdims=True)
        dq, first = None, 0
        for k_ref, v_ref, dk_sum, dv_sum in zip(k_refs, v_refs, dk_sums, dv_sums):
            count = k_ref.shape[0]
            p = p_ref[head, :, first : first + count]
            first += count
            ds = low(p.astype(F32) * (dot_nt(doz, v_ref[...]) - delta))
            dv_sum[rows, :] += dot(do_turned[rows], p)
            dk_sum[rows, :] += dot(q_turned[rows], ds)
            term = dot(ds, k_ref[...])
            dq = term if dq is None else dq + term
        dqs.append(dq)
    dq_ref[...] = low(jnp.where(lane_is(dqs[0].shape, 0), dqs[0], dqs[1]) * SELF_SCALE)

    @pl.when(step == steps - 1)
    def _():
        for ref, total in zip((*dk_refs, *dv_refs), (*dk_sums, *dv_sums)):
            ref[...] = jnp.transpose(low(total[...]))
        if comm is not None:
            for i in range(2):
                to_core(i, pair).start()

    if comm is not None:
        run_beside(comm, point + 1, SELF_PLAN, 1)

        @pl.when(point == 2 * (PAIRS * steps - 1))
        def _():
            for p in range(PAIRS):
                for i in range(2):
                    to_core(i, p).wait()


def self_backward(q2, do2, o2, scale2, p2, keys, values, comm=None):
    rows = q2.shape[0]
    block = min(rows, 256)
    parts = len(keys)
    whole = lambda array: (array, (array.shape[0], LANES), lambda p, i: (0, p))
    made = lambda array: (array.shape, BF16, (array.shape[0], LANES), lambda p, i: (0, p))
    if comm is None:
        outs, extra = [made(k) for k in keys] + [made(v) for v in values], []
    else:
        outs = [made(keys[0]), made(values[0])] + [((rows, D), BF16, None, None)] * 2
        extra = [pltpu.VMEM((2, PAIRS, rows, LANES), BF16)] + sem_pair(2, PAIRS)
    out = call(
        functools.partial(self_backward_kernel, parts, rows // block, comm),
        (PAIRS, rows // block),
        [
            (q2, (block, LANES), lambda p, i: (i, p)),
            (do2, (block, LANES), lambda p, i: (i, p)),
            (o2, (block, LANES), lambda p, i: (i, p)),
            (scale2, (block, LANES), lambda p, i: (i, p)),
            (p2, (2, block, p2.shape[2]), lambda p, i: (p, i, 0)),
        ]
        + [whole(k) for k in keys]
        + [whole(v) for v in values],
        [((rows, D), BF16, (block, LANES), lambda p, i: (i, p))] + outs,
        [pltpu.VMEM((LANES, k.shape[0]), F32) for k in (*keys, *values)] + extra,
        comm=comm,
        collective_id=1,
    )
    return out[0], out[1 : 1 + len(outs)], out[1 + len(outs) :]


def second_kernel(
    steps, x2_ref, o2_ref, og_ref, gain_ref, wso_ref, wup_ref, wdown_ref,
    out_ref, g3_ref, do_ref, dwup_ref, dwdown_ref, dwso_ref, dgain_ref,
    m_ref, f_ref, dm_ref,
):
    c = pl.program_id(0)

    @pl.when(c == 0)
    def _():
        x3 = x2_ref[...] + dot(o2_ref[...], wso_ref[...])
        unit, _ = normed(x3)
        m_ref[...] = low(unit * gain_ref[4:5, :])
        out_ref[...] = x3
        f_ref[...] = jnp.zeros_like(f_ref)
        dm_ref[...] = jnp.zeros_like(dm_ref)

    m, og = m_ref[...], og_ref[...]
    h, slope = gelu_both(dot(m, wup_ref[...]))
    h = low(h)
    f_ref[...] += dot(h, wdown_ref[...])
    dwdown_ref[...] = low(dot_tn(h, og))
    du = low(slope * dot_nt(og, wdown_ref[...]))
    dwup_ref[...] = low(dot_tn(m, du))
    dm_ref[...] += dot_nt(du, wup_ref[...])

    @pl.when(c == steps - 1)
    def _():
        x3 = out_ref[...]
        unit, factor = normed(x3)
        out_ref[...] = x3 + f_ref[...]
        back, dgain = norm_back(dm_ref[...], unit, factor, gain_ref[4:5, :])
        g3 = og_ref[...].astype(F32) + back
        g3_ref[...] = g3
        dgain_ref[...] = jnp.broadcast_to(dgain, dgain_ref.shape)
        b3 = low(g3)
        o2 = o2_ref[...]
        dwso_ref[...] = low(dot_tn(o2, b3))
        do_ref[...] = low(dot_nt(b3, wso_ref[...]))


def second(x2, o2, og, gains, so, up2, down2):
    rows = x2.shape[0]
    steps = FF // FF_STEP
    r = (rows, D)
    return call(
        functools.partial(second_kernel, steps),
        (steps,),
        [
            (x2, r, flat),
            (o2, r, flat),
            (og, r, flat),
            (gains, (8, D), flat),
            (so, (D, D), flat),
            (up2, (D, FF_STEP), lambda c: (0, c)),
            (down2, (FF_STEP, D), lambda c: (c, 0)),
        ],
        [
            (r, F32, r, flat),
            (r, F32, r, flat),
            (r, BF16, r, flat),
            ((D, FF), BF16, (D, FF_STEP), lambda c: (0, c)),
            ((FF, D), BF16, (FF_STEP, D), lambda c: (c, 0)),
            ((D, D), BF16, (D, D), flat),
            ((8, D), F32, (8, D), flat),
        ],
        [pltpu.VMEM(r, BF16), pltpu.VMEM(r, F32), pltpu.VMEM(r, F32)],
    )


def qkv_back_kernel(
    x2_ref, g3_ref, dq_ref, dk_ref, dk_more_ref, dv_ref, dv_more_ref, gain_ref, w_ref,
    g2_ref, dw_ref, dgain_ref,
):
    unit, factor = normed(x2_ref[...])
    gain = gain_ref[3:4, :]
    bn = low(unit * gain)
    dq = dq_ref[...]
    dk = low(dk_ref[...].astype(F32) + dk_more_ref[...].astype(F32))
    dv = low(dv_ref[...].astype(F32) + dv_more_ref[...].astype(F32))
    dbn = None
    for i, part in enumerate((dq, dk, dv)):
        cols = slice(i * D, (i + 1) * D)
        dw_ref[:, cols] = low(dot_tn(bn, part))
        term = dot_nt(part, w_ref[:, cols])
        dbn = term if dbn is None else dbn + term
    back, dgain = norm_back(dbn, unit, factor, gain)
    g2_ref[...] = g3_ref[...] + back
    dgain_ref[...] = jnp.broadcast_to(dgain, dgain_ref.shape)


def qkv_back(x2, g3, dq, dk, dk_more, dv, dv_more, gains, qkv):
    rows = x2.shape[0]
    r = (rows, D)
    return call(
        qkv_back_kernel,
        (1,),
        [(a, r, flat) for a in (x2, g3, dq, dk, dk_more, dv, dv_more)]
        + [(gains, (8, D), flat), (qkv, (D, 3 * D), flat)],
        [
            (r, F32, r, flat),
            ((D, 3 * D), BF16, (D, 3 * D), flat),
            ((8, D), F32, (8, D), flat),
        ],
    )


def first_back_kernel(
    steps, x1_ref, g2_ref, o_ref, gain_ref, wout_ref, wup_ref, wdown_ref,
    g1_ref, do_ref, dwup_ref, dwdown_ref, dwout_ref, dgain_ref,
    m_ref, b_ref, dm_ref,
):
    c = pl.program_id(0)

    @pl.when(c == 0)
    def _():
        unit, _ = normed(x1_ref[...])
        m_ref[...] = low(unit * gain_ref[2:3, :])
        b_ref[...] = low(g2_ref[...])
        dm_ref[...] = jnp.zeros_like(dm_ref)

    m, b = m_ref[...], b_ref[...]
    h, slope = gelu_both(dot(m, wup_ref[...]))
    dwdown_ref[...] = low(dot_tn(low(h), b))
    du = low(slope * dot_nt(b, wdown_ref[...]))
    dwup_ref[...] = low(dot_tn(m, du))
    dm_ref[...] += dot_nt(du, wup_ref[...])

    @pl.when(c == steps - 1)
    def _():
        unit, factor = normed(x1_ref[...])
        back, dgain = norm_back(dm_ref[...], unit, factor, gain_ref[2:3, :])
        g1 = g2_ref[...] + back
        g1_ref[...] = g1
        dgain_ref[...] = jnp.broadcast_to(dgain, dgain_ref.shape)
        b1 = low(g1)
        dwout_ref[...] = low(dot_tn(o_ref[...], b1))
        do_ref[...] = low(dot_nt(b1, wout_ref[...]))


def first_back(x1, g2, o, gains, mix, up1, down1):
    rows = x1.shape[0]
    steps = FF // FF_STEP
    r = (rows, D)
    return call(
        functools.partial(first_back_kernel, steps),
        (steps,),
        [
            (x1, r, flat),
            (g2, r, flat),
            (o, r, flat),
            (gains, (8, D), flat),
            (mix, (D, D), column(3)),
            (up1, (D, FF_STEP), lambda c: (0, c)),
            (down1, (FF_STEP, D), lambda c: (c, 0)),
        ],
        [
            (r, F32, r, flat),
            (r, BF16, r, flat),
            ((D, FF), BF16, (D, FF_STEP), lambda c: (0, c)),
            ((FF, D), BF16, (FF_STEP, D), lambda c: (c, 0)),
            ((D, D), BF16, (D, D), flat),
            ((8, D), F32, (8, D), flat),
        ],
        [pltpu.VMEM(r, BF16), pltpu.VMEM(r, BF16), pltpu.VMEM(r, F32)],
    )


def cross_back_kernel(
    steps, lat_ref, g1_ref, do_ref, p_ref, q_ref, kv_ref, gain_ref, wq_ref,
    lg_ref, dwq_ref, dkv_ref, dgain_ref, dk_sum, dv_sum, dwq_sum,
):
    i = pl.program_id(0)

    @pl.when(i == 0)
    def _():
        for ref in (dk_sum, dv_sum, dwq_sum, dgain_ref):
            ref[...] = jnp.zeros_like(ref)

    p, do, q = p_ref[...], do_ref[...], q_ref[...]
    dp = dot_nt(do, kv_ref[:, D:])
    wide_p = p.astype(F32)
    ds = low(wide_p * (dp - jnp.sum(wide_p * dp, axis=1, keepdims=True)))
    dq = low(dot(ds, kv_ref[:, :D]) * CROSS_SCALE)
    dk_sum[...] += dot_tn(ds, q)
    dv_sum[...] += dot_tn(p, do)
    unit, factor = normed(lat_ref[...].astype(F32))
    gain = gain_ref[0:1, :]
    dwq_sum[...] += dot_tn(low(unit * gain), dq)
    back, dgain = norm_back(dot_nt(dq, wq_ref[...]), unit, factor, gain)
    lg_ref[...] = g1_ref[...] + back
    dgain_ref[...] += jnp.broadcast_to(dgain, dgain_ref.shape)

    @pl.when(i == steps - 1)
    def _():
        dwq_ref[...] = low(dwq_sum[...])
        dkv_ref[:, :D] = low(dk_sum[...] * CROSS_SCALE)
        dkv_ref[:, D:] = low(dv_sum[...])


def cross_back(latents, g1, do, p, q, kv, gains, mix):
    rows, span = p.shape
    block = min(rows, 512)
    r = (block, D)
    return call(
        functools.partial(cross_back_kernel, rows // block),
        (rows // block,),
        [
            (latents, r, rows_of),
            (g1, r, rows_of),
            (do, r, rows_of),
            (p, (block, span), rows_of),
            (q, r, rows_of),
            (kv, (span, 2 * D), flat),
            (gains, (8, D), flat),
            (mix, (D, D), column(2)),
        ],
        [
            ((rows, D), F32, r, rows_of),
            ((D, D), BF16, (D, D), flat),
            ((span, 2 * D), BF16, (span, 2 * D), flat),
            ((8, D), F32, (8, D), flat),
        ],
        [pltpu.VMEM((span, D), F32), pltpu.VMEM((span, D), F32), pltpu.VMEM((D, D), F32)],
    )


def token_back_kernel(tok_ref, dkv_ref, more_ref, gain_ref, w_ref, tg_ref, dw_ref, dgain_ref):
    unit, factor = normed(tok_ref[...].astype(F32))
    gain = gain_ref[1:2, :]
    dkv = low(dkv_ref[...].astype(F32) + more_ref[...].astype(F32))
    dw_ref[...] = low(dot_tn(low(unit * gain), dkv))
    back, dgain = norm_back(dot_nt(dkv, w_ref[...]), unit, factor, gain)
    tg_ref[...] = low(back)
    dgain_ref[...] = jnp.broadcast_to(dgain, dgain_ref.shape)


def token_back(tokens, dkv, more, gains, mix):
    rows = tokens.shape[0]
    return call(
        token_back_kernel,
        (1,),
        [
            (tokens, (rows, D), flat),
            (dkv, (rows, 2 * D), flat),
            (more, (rows, 2 * D), flat),
            (gains, (8, D), flat),
            (mix, (D, 2 * D), column(0)),
        ],
        [
            ((rows, D), BF16, (rows, D), flat),
            ((D, 2 * D), BF16, (D, 2 * D), flat),
            ((8, D), F32, (8, D), flat),
        ],
    )


MESH = pl.DeviceIdType.MESH
UP, DOWN = 0, 1


class Place:
    def __init__(self):
        row, lat = lax.axis_index("row"), lax.axis_index("lat")
        self.x, self.y, self.z, self.c = row % 2, row // 2, lat // 2, lat % 2
        self.r = row
        self.rx = self.y * 2 + 1 - self.x
        self.ry = (1 - self.y) * 2 + self.x
        self.rd = (1 - self.y) * 2 + 1 - self.x
        self.to_x, self.to_y = (self.rx, lat), (self.ry, lat)
        self.to_core = (row, self.z * 2 + 1 - self.c)
        self.to_z = ((row, lat + 2), (row, lat - 2))
        self.more = (self.z < 3, self.z > 0)

    def greet(self):
        barrier = pltpu.get_barrier_semaphore()
        for device in (self.to_x, self.to_y, self.to_core):
            pl.semaphore_signal(barrier, inc=1, device_id=device, device_id_type=MESH)
        for way in (UP, DOWN):
            @pl.when(self.more[way])
            def _():
                pl.semaphore_signal(barrier, inc=1, device_id=self.to_z[way], device_id_type=MESH)
        pl.semaphore_wait(barrier, 3 + jnp.minimum(self.z, 1) + jnp.minimum(3 - self.z, 1))

    def source(self, way, hop):
        return (self.z - hop, self.z >= hop) if way == UP else (self.z + hop, self.z + hop <= 3)


def send(src, dst, sems, index, device):
    return pltpu.make_async_remote_copy(
        src_ref=src, dst_ref=dst, send_sem=sems[0].at[index], recv_sem=sems[1].at[index],
        device_id=device, device_id_type=MESH,
    )


def sem_pair(*shape):
    return [pltpu.SemaphoreType.DMA(shape), pltpu.SemaphoreType.DMA(shape)]


TOKEN_PARTS = 4
AHEAD = 2
GAP = 2
SHIFT = 3
WEIGHT, TOKENS, NOTES = range(3)


class Gather:
    def __init__(self, weights, tokens=None, notes=()):
        self.inputs, self.out_shapes, self.chunks = [], [], []
        self.shards = []
        for shards in weights:
            shape = (4, shards[0].shape[0] // 4)
            self.shards.append([])
            for shard in shards:
                self.shards[-1].append((len(self.inputs), shard.shape[1]))
                self.inputs.append(shard.reshape(shape + shard.shape[1:]))
            cols = sum(shard.shape[1] for shard in shards)
            self.out_shapes.append(jax.ShapeDtypeStruct((4, 2) + shape + (cols,), BF16))
        self.chunks = [(WEIGHT, k) for k in range(len(weights))]
        self.out_specs = [ANYWHERE] * len(weights)
        self.copies = len(self.inputs)
        self.scratch = []
        self.noted = len(notes)
        if tokens is not None:
            self.inputs += [tokens, *notes]
            self.out_shapes += [
                jax.ShapeDtypeStruct((4, 2) + tokens.shape, BF16),
                jax.ShapeDtypeStruct((8, tokens.shape[0]), BF16),
                jax.ShapeDtypeStruct((8, D), F32),
            ]
            self.out_specs += [ANYWHERE] + [inside(made.shape) for made in self.out_shapes[-2:]]
            self.chunks = [(NOTES, 0)] + self.chunks + [(TOKENS, k) for k in range(TOKEN_PARTS)]
            self.scratch.append(pltpu.VMEM((4, 2, 16, tokens.shape[0]), BF16))
            self.copies += 1
        self.in_specs = [inside(array.shape) for array in self.inputs]
        n = len(self.chunks)
        self.scratch += [pltpu.SemaphoreType.DMA((self.copies,))]
        for shape in ((n, 2, 3), (n, 2, 3, 2), (n, 2, 3, 2), (n, 7)):
            self.scratch += sem_pair(*shape)
        self.steps = n + 4 * GAP + 1

    def bind(self, ins, outs, scratch):
        self.here, self.ins, self.outs = Place(), ins, outs
        scratch = list(scratch)
        take = lambda n: [scratch.pop(0) for _ in range(n)]
        if self.noted:
            self.notes = take(1)[0]
        self.local = take(1)[0]
        self.z_sems, self.p_sems, self.q_sems, self.c_sems = (take(2) for _ in range(4))

    def block(self, k, source, core=None):
        kind, index = self.chunks[k]
        core = self.here.c if core is None else core
        if kind == NOTES:
            return self.notes.at[source, core]
        if kind == TOKENS:
            tokens = self.outs[len(self.shards)]
            rows = tokens.shape[2] // TOKEN_PARTS
            return tokens.at[source, core, pl.ds(index * rows, rows)]
        return self.outs[index].at[source, core]

    def piece(self, k, source, quarter, half=None):
        if not self.shared(k):
            return self.block(k, source)
        ref = self.outs[self.chunks[k][1]]
        if half is None:
            return ref.at[source, self.here.c, quarter]
        width = ref.shape[-1] // 2
        return ref.at[source, self.here.c, quarter, :, pl.ds(half * width, width)]

    def shared(self, k):
        return self.chunks[k][0] == WEIGHT

    def z_send(self, k, way, hop):
        source, _ = self.here.source(way, hop - 1)
        ref = self.piece(k, source, self.here.r)
        return send(ref, ref, self.z_sems, (k, way, hop - 1), self.here.to_z[way])

    def z_recv(self, k, way, hop):
        source, _ = self.here.source(way, hop)
        ref = self.piece(k, source, self.here.r)
        return send(ref, ref, self.z_sems, (k, way, hop - 1), self.here.to_z[way])

    def p_copy(self, k, way, hop, axis, mine):
        here = self.here
        source, _ = here.source(way, hop)
        ref = self.piece(k, source, here.r if mine else (here.rx, here.ry)[axis])
        return send(ref, ref, self.p_sems, (k, way, hop - 1, axis), (here.to_x, here.to_y)[axis])

    def q_copy(self, k, way, hop, half, mine):
        here = self.here
        source, _ = here.source(way, hop)
        ref = self.piece(k, source, (here.rx, here.ry)[half] if mine else here.rd, half)
        return send(ref, ref, self.q_sems, (k, way, hop - 1, half), (here.to_y, here.to_x)[half])

    def c_copy(self, k, source, index, mine):
        ref = self.block(k, source, self.here.c if mine else 1 - self.here.c)
        return send(ref, ref, self.c_sems, (k, index), self.here.to_core)

    def ways(self, hop, fn):
        for way in (UP, DOWN):
            source, valid = self.here.source(way, hop)
            pl.when(valid)(functools.partial(fn, way, hop, source))

    @staticmethod
    def index_of(way, hop):
        return 1 + way * 3 + hop - 1

    def first_sends(self, k):
        for way in (UP, DOWN):
            pl.when(self.here.more[way])(lambda way=way: self.z_send(k, way, 1).start())
        self.c_copy(k, self.here.z, 0, True).start()

    def stage_z(self, k, hop):
        def arrive(way, hop, source):
            self.z_recv(k, way, hop).wait_recv()
            if hop < 3:
                pl.when(self.here.more[way])(lambda: self.z_send(k, way, hop + 1).start())
            if self.shared(k):
                self.p_copy(k, way, hop, 0, True).start()
                self.p_copy(k, way, hop, 1, True).start()
            else:
                self.c_copy(k, source, self.index_of(way, hop), True).start()
        self.ways(hop, arrive)

    def stage_p(self, k, hop):
        def arrive(way, hop, source):
            for axis in (0, 1):
                self.p_copy(k, way, hop, axis, False).wait_recv()
                self.q_copy(k, way, hop, axis, True).start()
        self.ways(hop, arrive)

    def stage_q(self, k, hop):
        def arrive(way, hop, source):
            self.q_copy(k, way, hop, 0, False).wait_recv()
            self.q_copy(k, way, hop, 1, False).wait_recv()
            self.c_copy(k, source, self.index_of(way, hop), True).start()
        self.ways(hop, arrive)

    def local_copies(self):
        z, c = self.here.z, self.here.c
        copies = []
        for k, shards in enumerate(self.shards):
            first = 0
            for index, width in shards:
                copies.append(pltpu.make_async_copy(
                    self.ins[index], self.outs[k].at[z, c, :, :, pl.ds(first, width)],
                    self.local.at[len(copies)]))
                first += width
        if self.noted:
            copies.append(pltpu.make_async_copy(
                self.ins[len(copies)], self.outs[len(self.shards)].at[z, c], self.local.at[len(copies)]))
        return copies

    def begin(self):
        for copy in self.local_copies():
            copy.start()
        if self.noted:
            z, c = self.here.z, self.here.c
            scenes, mask, *gains = self.ins[self.copies :]
            self.notes[z, c] = jnp.zeros(self.notes.shape[2:], BF16)
            self.notes[z, c, 0:1, :] = low(jnp.where(mask[...] == 1, scenes[...], -1).astype(F32))
            for i, gain in enumerate(gains):
                self.notes[z, c, 1 + i : 2 + i, : gain.shape[1]] = gain[...]

    def begin_sends(self):
        for copy in self.local_copies():
            copy.wait()
        for k in range(min(AHEAD, len(self.chunks))):
            self.first_sends(k)

    def step(self, step):
        total = len(self.chunks)
        if step + AHEAD < total:
            self.first_sends(step + AHEAD)
        for lag, stage in ((0, self.stage_z), (GAP, self.stage_p), (2 * GAP, self.stage_q)):
            for hop in (1, 2, 3):
                k = step - lag - GAP * (hop - 1)
                if 0 <= k < total and (lag == 0 or self.shared(k)):
                    stage(k, hop)

    def finish(self):
        here = self.here
        for k in range(len(self.chunks)):
            for way in (UP, DOWN):
                for hop in (1, 2, 3):
                    _, valid = here.source(way, hop - 1)
                    pl.when(valid & here.more[way])(
                        lambda k=k, way=way, hop=hop: self.z_send(k, way, hop).wait_send())
            self.c_copy(k, here.z, 0, True).wait_send()
            self.c_copy(k, here.z, 0, False).wait_recv()

            def settle(way, hop, source):
                self.c_copy(k, source, self.index_of(way, hop), True).wait_send()
                self.c_copy(k, source, self.index_of(way, hop), False).wait_recv()
                if self.shared(k):
                    for axis in (0, 1):
                        self.p_copy(k, way, hop, axis, True).wait_send()
                        self.q_copy(k, way, hop, axis, True).wait_send()
            for hop in (1, 2, 3):
                self.ways(hop, settle)
        if self.noted:
            tags, gains = self.outs[-2:]
            width = D // 8
            gains[...] = jnp.zeros_like(gains)
            for i in range(8):
                tags[i : i + 1, :] = self.notes[i // 2, i % 2, 0:1, :]
                for j in range(5):
                    gains[j : j + 1, i * width : (i + 1) * width] = self.notes[
                        i // 2, i % 2, 1 + j : 2 + j, :width
                    ].astype(F32)


def gather_kernel(comm, *refs):
    n_in, n_out = len(comm.inputs), len(comm.out_shapes)
    comm.bind(refs[:n_in], refs[n_in : n_in + n_out], refs[n_in + n_out :])
    comm.here.greet()
    comm.begin()
    comm.begin_sends()
    for step in range(comm.steps):
        comm.step(step)
    comm.finish()


def gather_now(comm):
    return call(functools.partial(gather_kernel, comm), (1,), [], [], comm=comm, collective_id=0)


class Peers(Place):
    def __init__(self):
        super().__init__()
        lat = lax.axis_index("lat")
        self.plane = (self.to_x, self.to_y, (self.rd, lat))
        self.quarters = (self.rx, self.ry, self.rd)
        self.above = [lax.rem(self.z + 1 + i, 4) for i in range(3)]
        self.line = [(self.r, z * 2 + self.c) for z in self.above]

    def greet(self):
        barrier = pltpu.get_barrier_semaphore()
        others = (self.to_core, *self.plane, *self.line)
        for device in others:
            pl.semaphore_signal(barrier, inc=1, device_id=device, device_id_type=MESH)
        pl.semaphore_wait(barrier, len(others))


LINE = (
    ((1, UP, 3), (2, DOWN, 0)),
    ((1, UP, 2), (2, DOWN, 1), (2, UP, 3), (1, DOWN, 0)),
    ((1, UP, 1), (2, DOWN, 2), (2, UP, 2), (1, DOWN, 1)),
    ((3, UP, 3), (0, DOWN, 0)),
)


class LineSum:
    def __init__(self, here, block, arrived, sems):
        self.here, self.block, self.arrived, self.sems = here, block, arrived, sems

    def copy(self, way, dest):
        index = (way, dest - 1 if way == UP else dest)
        return send(self.block(dest), self.arrived.at[index], [s for s in self.sems], index, self.here.to_z[way])

    def start(self):
        @pl.when(self.here.z == 0)
        def _():
            for dest in (3, 2, 1):
                self.copy(UP, dest).start()

        @pl.when(self.here.z == 3)
        def _():
            for dest in (0, 1, 2):
                self.copy(DOWN, dest).start()

    def turn(self, group):
        for device, way, dest in LINE[group]:
            @pl.when(self.here.z == device)
            def _(device=device, way=way, dest=dest):
                self.copy(way, dest).wait_recv()
                ref = self.block(dest)
                ref[...] = ref[...] + self.arrived[way, dest - 1 if way == UP else dest]
                if dest != device:
                    self.copy(way, dest).start()

    def finish(self):
        for dest in (1, 2, 3):
            pl.when(self.here.z < dest)(lambda dest=dest: self.copy(UP, dest).wait_send())
        for dest in (0, 1, 2):
            pl.when(self.here.z > dest)(lambda dest=dest: self.copy(DOWN, dest).wait_send())


class Staged:
    def __init__(self, rows, cols):
        self.shape = (rows, cols)


class WeightSum:
    def __init__(self, chunks, gains=None, tokens=None):
        self.chunks, self.inputs, self.scratch, self.staged = [], [], [], []
        self.sources = 0
        for chunk in chunks:
            parts = []
            for array in chunk:
                shape = (4, 2, 4, array.shape[0] // 32, array.shape[1])
                if isinstance(array, Staged):
                    parts.append((self.sources, None, len(self.staged), shape[-1]))
                    self.staged.append(pltpu.VMEM(shape, BF16))
                else:
                    parts.append((self.sources, len(self.inputs), None, shape[-1]))
                    self.inputs.append(array.reshape(shape))
                self.sources += 1
            self.chunks.append((parts, shape[3], sum(part[3] for part in parts)))
        self.out_shapes = [
            jax.ShapeDtypeStruct((4, rows, cols), BF16) for _, rows, cols in self.chunks
        ]
        for _, rows, cols in self.chunks:
            half = cols // 2
            self.scratch += [
                pltpu.VMEM((4, 2, 2, rows, cols), BF16),
                pltpu.VMEM((4, 2, 2, rows, cols), BF16),
                pltpu.VMEM((2, 4, 2, rows, half), BF16),
                pltpu.VMEM((2, 4, rows, half), BF16),
                pltpu.VMEM((2, 3, rows, cols), BF16),
                pltpu.VMEM((4, rows, cols), BF16),
            ]
        n = len(self.chunks)
        self.scratch += self.staged
        self.scratch += [pltpu.SemaphoreType.DMA((self.sources, 2))]
        for shape in ((self.sources, 2), (n, 2), (n, 2), (n, 2, 3), (n, 3)):
            self.scratch += sem_pair(*shape)
        self.gains, self.tokens = gains, tokens
        if gains is not None:
            self.out_shapes.append(jax.ShapeDtypeStruct(gains, F32))
            self.scratch += [pltpu.VMEM(shape + gains, F32) for shape in ((), (), (4,), (3,))]
            self.scratch += sem_pair(1) + sem_pair(3) + sem_pair(3)
        if tokens is not None:
            self.out_shapes.append(jax.ShapeDtypeStruct((tokens // 8, D), BF16))
            self.scratch += [pltpu.VMEM((4, tokens // 8, D), BF16)]
            self.scratch += [pltpu.VMEM((2, tokens // 8, D), BF16)]
            self.scratch += [pltpu.VMEM((2, 3, tokens // 8, D), BF16)]
            self.scratch += sem_pair(1) + sem_pair(2, 3)
        self.in_specs = [ANYWHERE] * len(self.inputs)
        self.out_specs = [inside(made.shape) for made in self.out_shapes]

    def bind(self, ins, outs, scratch):
        self.here = Peers()
        self.ins, self.outs = ins, outs
        scratch = list(scratch)
        take = lambda n: [scratch.pop(0) for _ in range(n)]
        self.buffers = [take(6) for _ in self.chunks]
        self.stages = take(len(self.staged))
        self.local = take(1)[0]
        self.c_sems, self.x_sems, self.y_sems, self.z_sems, self.g_sems = (take(2) for _ in range(5))
        if self.gains is not None:
            self.gain_buffers = take(4)
            self.gain_sems = [take(2) for _ in range(3)]
        if self.tokens is not None:
            self.token_mine, self.token_window, arrived = take(3)
            self.token_sems = take(2)
            self.token_line = LineSum(self.here, lambda z: self.token_mine.at[z], arrived, take(2))


    def parts(self, k):
        first = 0
        for source, given, staged, width in self.chunks[k][0]:
            ref = self.stages[staged] if given is None else self.ins[given]
            yield source, ref, pl.ds(first, width)
            first += width

    def halves(self, k):
        half = self.chunks[k][2] // 2
        return pl.ds(0, half), pl.ds(half, half)

    def own(self, k):
        for source, ref, cols in self.parts(k):
            for y in range(2):
                yield pltpu.make_async_copy(
                    ref.at[:, self.here.c, pl.ds(2 * y, 2)],
                    self.buffers[k][0].at[:, y, :, :, cols],
                    self.local.at[source, y],
                )

    def to_core(self, k):
        for source, ref, cols in self.parts(k):
            for y in range(2):
                yield send(
                    ref.at[:, 1 - self.here.c, pl.ds(2 * y, 2)],
                    self.buffers[k][1].at[:, y, :, :, cols],
                    self.c_sems, (source, y), self.here.to_core,
                )

    def first_turn(self, k):
        mine, theirs, here = self.buffers[k][0], self.buffers[k][2], self.here
        left, right = self.halves(k)
        yield send(mine.at[:, :, 1 - here.x, :, left], theirs.at[0], self.x_sems, (k, 0), here.to_x)
        yield send(mine.at[:, 1 - here.y, :, :, right], theirs.at[1], self.x_sems, (k, 1), here.to_y)

    def second_turn(self, k):
        mine, theirs, here = self.buffers[k][0], self.buffers[k][3], self.here
        left, right = self.halves(k)
        yield send(mine.at[:, 1 - here.y, here.x, :, left], theirs.at[0], self.y_sems, (k, 0), here.to_y)
        yield send(mine.at[:, here.y, 1 - here.x, :, right], theirs.at[1], self.y_sems, (k, 1), here.to_x)

    def line(self, k):
        here, buffers = self.here, self.buffers[k]
        sems = [sem.at[k] for sem in self.z_sems]
        return LineSum(here, lambda z: buffers[0].at[z, here.y, here.x], buffers[4], sems)

    def finished(self, k):
        for i in range(3):
            mine = self.buffers[k][5].at[self.here.r]
            yield send(mine, mine, self.g_sems, (k, i), self.here.plane[i])

    def arriving(self, k):
        for i in range(3):
            theirs = self.buffers[k][5].at[self.here.quarters[i]]
            yield send(theirs, theirs, self.g_sems, (k, i), self.here.plane[i])


    def start(self, k):
        for copy in (*self.own(k), *self.to_core(k)):
            copy.start()

    def in_chip(self, k):
        for copy in self.own(k):
            copy.wait()
        for copy in self.to_core(k):
            copy.wait_recv()
        mine, theirs = self.buffers[k][:2]
        for z in range(4):
            for y in range(2):
                for x in range(2):
                    mine[z, y, x] = mine[z, y, x] + theirs[z, y, x]
        for copy in self.first_turn(k):
            copy.start()

    def in_pairs(self, k):
        for copy in self.first_turn(k):
            copy.wait()
        mine, theirs, here = self.buffers[k][0], self.buffers[k][2], self.here
        left, right = self.halves(k)
        for z in range(4):
            for i in range(2):
                mine[z, i, here.x, :, left] = mine[z, i, here.x, :, left] + theirs[0, z, i]
                mine[z, here.y, i, :, right] = mine[z, here.y, i, :, right] + theirs[1, z, i]
        for copy in self.second_turn(k):
            copy.start()

    def in_plane(self, k):
        for copy in self.second_turn(k):
            copy.wait()
        mine, theirs, here = self.buffers[k][0], self.buffers[k][3], self.here
        for z in range(4):
            for i, cols in enumerate(self.halves(k)):
                mine[z, here.y, here.x, :, cols] = mine[z, here.y, here.x, :, cols] + theirs[i, z]
        self.line(k).start()

    def turn0(self, k):
        self.line(k).turn(0)

    def turn1(self, k):
        self.line(k).turn(1)

    def turn2(self, k):
        self.line(k).turn(2)

    def in_line(self, k):
        self.line(k).turn(3)
        mine, done, here = self.buffers[k][0], self.buffers[k][5], self.here
        done[here.r] = mine[here.z, here.y, here.x]
        for copy in self.finished(k):
            copy.start()

    def end(self, k):
        for copy in self.arriving(k):
            copy.wait_recv()
        for copy in (*self.to_core(k), *self.finished(k)):
            copy.wait_send()
        self.line(k).finish()
        self.outs[k][...] = self.buffers[k][5][...]


    def gain_copy(self, stage, i):
        mine, core, plane, line = self.gain_buffers
        if stage == 0:
            return send(mine, core, self.gain_sems[0], 0, self.here.to_core)
        if stage == 1:
            return send(mine, plane.at[self.here.r], self.gain_sems[1], i, self.here.plane[i])
        return send(mine, line.at[i], self.gain_sems[2], i, self.here.line[i])

    def gain_plane_recv(self, i):
        mine, _, plane, _ = self.gain_buffers
        return send(mine, plane.at[self.here.quarters[i]], self.gain_sems[1], i, self.here.plane[i])

    def gain_step(self, stage):
        mine, core, plane, line = self.gain_buffers
        if stage == 0:
            self.gain_copy(0, 0).start()
        elif stage == 1:
            self.gain_copy(0, 0).wait()
            mine[...] += core[...]
            plane[self.here.r] = mine[...]
            for i in range(3):
                self.gain_copy(1, i).start()
        elif stage == 2:
            for i in range(3):
                self.gain_copy(1, i).wait_send()
                self.gain_plane_recv(i).wait_recv()
            mine[...] = (plane[0] + plane[1]) + (plane[2] + plane[3])
            for i in range(3):
                self.gain_copy(2, i).start()
        else:
            for i in range(3):
                self.gain_copy(2, i).wait()
            self.outs[len(self.chunks)][...] = (mine[...] + line[0]) + (line[1] + line[2])


    def token_core(self):
        mine = self.token_window.at[self.here.c]
        return send(mine, mine, self.token_sems, 0, self.here.to_core)

    def token_core_recv(self):
        theirs = self.token_window.at[1 - self.here.c]
        return send(theirs, theirs, self.token_sems, 0, self.here.to_core)

    def token_place(self, start):
        self.token_core().wait_send()
        self.token_core_recv().wait_recv()
        count, rows = 2 * self.token_window.shape[1], self.token_mine.shape[1]
        window = self.token_window[...].reshape(count, D)
        for z in range(4):
            slot = lax.broadcasted_iota(jnp.int32, (rows, count), 0) + (2 * z + self.here.c) * rows
            row = lax.broadcasted_iota(jnp.int32, (rows, count), 1) + start
            self.token_mine[z] = low(dot(low(jnp.where(slot == row, 1.0, 0.0)), window))
        self.token_line.start()

    def token_end(self):
        self.token_line.turn(3)
        self.outs[-1][...] = self.token_mine[self.here.z]
        self.token_line.finish()


def tail_kernel(
    comm, lat_ref, do_ref, p_ref, q_ref, kv_ref, gain_ref, wq_ref, wkv_ref, win_ref, start_ref,
    dm1_ref, ds_ref, dm2_ref, *refs,
):
    n_in, n_out = len(comm.inputs), len(comm.out_shapes)
    ins, lg_ref = refs[:n_in], refs[n_in]
    outs, scratch = refs[n_in + 1 : n_in + 1 + n_out], refs[n_in + 1 + n_out :]
    kv_sum, dkv_ref, more_ref, kv_sems = scratch[0], scratch[1], scratch[2], scratch[3:5]
    comm.bind(ins, outs, scratch[5:])
    here = comm.here
    mixed = len(comm.chunks) - 1
    early = range(mixed)
    rows, span = p_ref.shape
    gains = comm.gain_buffers[0]

    here.greet()
    for k in early:
        comm.start(k)
    block = rows // 2
    dwq = None
    gains[...] = jnp.zeros_like(gains)
    for i in range(2):
        at = slice(i * block, (i + 1) * block)
        p, do, q = p_ref[at], do_ref[at], q_ref[at]
        dp = dot_nt(do, kv_ref[:, D:])
        wide_p = p.astype(F32)
        ds = low(wide_p * (dp - jnp.sum(wide_p * dp, axis=1, keepdims=True)))
        dq = low(dot(ds, kv_ref[:, :D]) * CROSS_SCALE)
        dk, dv = dot_tn(ds, q), dot_tn(p, do)
        if i == 0:
            kv_sum[:, :D], kv_sum[:, D:] = dk, dv
        else:
            dkv_ref[:, :D] = low((kv_sum[:, :D] + dk) * CROSS_SCALE)
            dkv_ref[:, D:] = low(kv_sum[:, D:] + dv)
        unit, factor = normed(lat_ref[at].astype(F32))
        gain = gain_ref[0:1, :]
        term = dot_tn(low(unit * gain), dq)
        dwq = term if dwq is None else dwq + term
        back, dgain = norm_back(dot_nt(dq, wq_ref[...]), unit, factor, gain)
        lg_ref[at] = low(back)
        gains[0:1] += dgain
        if i < mixed:
            comm.in_chip(i)
    for k in range(2, mixed):
        comm.in_chip(k)
    half = span // 2
    to_core = send(
        dkv_ref.at[pl.ds(half * (1 - here.c), half)], more_ref, kv_sems, 0, here.to_core)
    to_core.start()
    comm.stages[1][...] = low(dwq).reshape(comm.stages[1].shape)
    gains[2:3], gains[3:4], gains[4:5] = dm1_ref[0:1], ds_ref[0:1], dm2_ref[0:1]
    unit, factor = normed(win_ref[pl.ds(half * here.c, half)].astype(F32))
    gain = gain_ref[1:2, :]
    to_core.wait()
    dkv = low(dkv_ref[pl.ds(half * here.c, half)].astype(F32) + more_ref[...].astype(F32))
    back, dgain = norm_back(dot_nt(dkv, wkv_ref[...]), unit, factor, gain)
    comm.token_window[here.c] = low(back)
    comm.token_core().start()
    gains[1:2] = dgain
    comm.gain_step(0)
    comm.stages[0][...] = low(dot_tn(low(unit * gain), dkv)).reshape(comm.stages[0].shape)
    comm.start(mixed)
    comm.token_place(start_ref[0:1, 0:1])
    for k in early:
        comm.in_pairs(k)
    comm.in_chip(mixed)
    comm.gain_step(1)
    comm.token_line.turn(0)
    for k in early:
        comm.in_plane(k)
    comm.in_pairs(mixed)
    for k in early:
        comm.turn0(k)
    comm.token_line.turn(1)
    for k in early:
        comm.turn1(k)
    comm.in_plane(mixed)
    comm.gain_step(2)
    for k in early:
        comm.turn2(k)
    comm.turn0(mixed)
    comm.token_line.turn(2)
    for k in early:
        comm.in_line(k)
    comm.turn1(mixed)
    comm.gain_step(3)
    comm.turn2(mixed)
    comm.token_end()
    comm.in_line(mixed)
    for k in range(mixed + 1):
        comm.end(k)


def tail(comm, latents, do, p, q, kv, gains, mix, window, start, dgains):
    rows, span = p.shape
    r = (rows, D)
    return call(
        functools.partial(tail_kernel, comm),
        (1,),
        [
            (latents, r, flat),
            (do, r, flat),
            (p, p.shape, flat),
            (q, r, flat),
            (kv, kv.shape, flat),
            (gains, (8, D), flat),
            (mix, (D, D), column(2)),
            (mix, (D, 2 * D), column(0)),
            (window, (span, D), flat),
            (start, start.shape, flat),
        ]
        + [(g, (8, D), flat) for g in dgains],
        [(r, BF16, r, flat)],
        [
            pltpu.VMEM((span, 2 * D), F32),
            pltpu.VMEM((span, 2 * D), BF16),
            pltpu.VMEM((span // 2, 2 * D), BF16),
        ]
        + sem_pair(1),
        comm=comm,
        collective_id=2,
    )


def widen_kernel(cuts, base_ref, term_ref, *refs):
    sources, (sum_ref, *targets) = refs[: len(cuts)], refs[len(cuts) :]
    sum_ref[...] = base_ref[...] + term_ref[...].astype(F32)
    for source, widths in zip(sources, cuts):
        first = 0
        for width in widths:
            targets.pop(0)[...] = source[:, first : first + width].astype(F32)
            first += width


def widen(base, term, arrays, cuts):
    steps = 4
    rows = lambda array: array.shape[0] // steps
    return call(
        functools.partial(widen_kernel, cuts),
        (steps,),
        [(a, (rows(a), a.shape[1]), rows_of) for a in (base, term, *arrays)],
        [(base.shape, F32, (rows(base), base.shape[1]), rows_of)]
        + [
            ((a.shape[0], width), F32, (rows(a), width), rows_of)
            for a, widths in zip(arrays, cuts)
            for width in widths
        ],
    )


def from_partner(shard, bit):
    return lax.ppermute(shard, "lat", [(i, i ^ 1 << bit) for i in range(lax.axis_size("lat"))])


def gather_lat(shard):
    return lax.all_gather(shard, "lat", axis=0, tiled=True)


def halve(value, place, bits):
    kept, more = value, jnp.zeros_like(value)
    for bit in reversed(range(bits)):
        value = low(kept.astype(F32) + more.astype(F32))
        half = value.shape[0] // 2
        upper = place // 2**bit % 2
        kept = lax.dynamic_slice_in_dim(value, upper * half, half)
        more = from_partner(lax.dynamic_slice_in_dim(value, (1 - upper) * half, half), bit)
    return kept, more


def reduce_weights(grad):
    share = lax.psum_scatter(grad, "lat", scatter_dimension=0, tiled=True)
    return lax.psum(share, "row").astype(F32)


def local(
    tokens, latents, segment_ids, pad_mask, block_scene, out_grad,
    gain_cross_q, gain_cross_kv, w_cross_q, w_cross_kv, w_cross_out,
    gain_mlp1, w_up1, w_down1, gain_self, w_self_qkv, w_self_out, gain_mlp2, w_up2, w_down2,
):
    tokens, latents, og = tokens[0], latents[0], out_grad[0]
    rows, slots = latents.shape[0], tokens.shape[0] * lax.axis_size("lat")
    scenes = block_scene.shape[1]
    span = slots // scenes
    place = lax.axis_index("lat")
    group = LAT_SCENE // rows
    bits = group.bit_length() - 1

    block = place * rows // LAT_SCENE
    scene = jnp.sum(jnp.where(jnp.arange(scenes) == block, block_scene[0], 0))
    scene = jnp.broadcast_to(scene, (8, LANES))
    gains = [gain_cross_q, gain_cross_kv, gain_mlp1, gain_self, gain_mlp2]
    first_weights = [[w_cross_kv, w_cross_q, w_cross_out], [w_up1], [w_down1], [w_self_qkv]]
    later_weights = [[w_up2], [w_down2], [w_self_out]]
    planes = lax.axis_size("row") == 4 and lax.axis_size("lat") == 8 and group == 2
    join = lambda gathered: [w.reshape(-1, w.shape[-1]) for w in gathered]
    if planes:
        notes = [segment_ids, pad_mask] + [g.reshape(1, -1) for g in gains]
        *weights, all_tokens, tags, gains = gather_now(Gather(first_weights, tokens, notes))
        mix, up1, down1, qkv, all_tokens = join([*weights, all_tokens])
    else:
        tag = jnp.where(pad_mask == 1, segment_ids, -1)
        tags = gather_lat(low(tag))
        all_tokens = gather_lat(tokens)
        gains = lax.all_gather(jnp.stack(gains), "lat", axis=1, tiled=True)
        gains = jnp.pad(gains.astype(F32), ((0, 3), (0, 0)))
        mix, up1, down1, qkv, up2, down2, so = (
            gather_lat(jnp.concatenate(shards, axis=1)) for shards in first_weights + later_weights
        )

    x1, x2, q, p, o, kv, q2, k2, v2, window, start = front(
        latents, all_tokens, tags, scene, span, gains, mix, up1, down1, qkv
    )
    if planes:
        o2, p2, scale2, k2_more, v2_more, *weights = self_forward(q2, (k2,), (v2,), Gather(later_weights))
        up2, down2, so = join(weights)
        keys, values = (k2, k2_more), (v2, v2_more)
    else:
        for bit in range(bits):
            upper = place // 2**bit % 2 == 1
            more = from_partner((k2, v2), bit)
            k2, v2 = (
                jnp.where(upper, jnp.concatenate([b, a]), jnp.concatenate([a, b]))
                for a, b in zip((k2, v2), more)
            )
        keys, values = (k2,), (v2,)
        o2, p2, scale2 = self_forward(q2, keys, values)
    out, g3, do2, dwup2, dwdown2, dwso, dgain_m2 = second(x2, o2, og, gains, so, up2, down2)
    comm = WeightSum([[dwup2], [dwdown2], [dwso]]) if planes else None
    dq2, dkv2, early = self_backward(q2, do2, o2, scale2, p2, keys, values, comm)
    if planes:
        dk, dv, dk_more, dv_more = dkv2
    else:
        dk, dk_more = halve(dkv2[0], place, bits)
        dv, dv_more = halve(dkv2[1], place, bits)
    g2, dwqkv, dgain_s = qkv_back(x2, g3, dq2, dk, dk_more, dv, dv_more, gains, qkv)
    g1, do, dwup1, dwdown1, dwout, dgain_m1 = first_back(x1, g2, o, gains, mix, up1, down1)
    if planes:
        comm = WeightSum(
            [[dwqkv], [dwup1], [dwdown1], [Staged(D, 2 * D), Staged(D, D), dwout]], gains=(8, D), tokens=slots
        )
        term, *late, dgains, token_grad = tail(
            comm, latents, do, p, q, kv, gains, mix, window, start, (dgain_m1, dgain_s, dgain_m2)
        )
        dgains = lax.dynamic_slice_in_dim(dgains, place * (D // 8), D // 8, axis=1)
        up2, down2, so, qkv, up1, down1, mixed = join([*early, *late])
        latent_grad, token_grad, dwkv, dwq, dwout, *others = widen(
            g1, term, [token_grad, mixed, up1, down1, qkv, so, up2, down2],
            ((D,), (2 * D, D, D), (FF,), (D,), (3 * D,), (D,), (FF,), (D,)),
        )
        sums = dwq, dwkv, dwout, *others
    else:
        latent_grad, dwq, dkv, dgain_q = cross_back(latents, g1, do, p, q, kv, gains, mix)
        mine, more = halve(dkv, place, bits)
        first = place % group * (span // group)
        token_rows = lax.dynamic_slice_in_dim(window, first, span // group)
        token_part, dwkv, dgain_kv = token_back(token_rows, mine, more, gains, mix)
        token_part = lax.dynamic_update_slice_in_dim(
            jnp.zeros((slots, D), BF16), token_part, start[0, 0] + first, 0
        )
        token_grad = lax.psum_scatter(token_part, "lat", scatter_dimension=0, tiled=True).astype(F32)
        dgains = jnp.stack([g[0] for g in (dgain_q, dgain_kv, dgain_m1, dgain_s, dgain_m2)])
        dgains = lax.psum_scatter(low(dgains), "lat", scatter_dimension=1, tiled=True)
        dgains = lax.psum(dgains, "row").astype(F32)
        sums = [
            reduce_weights(g) for g in (dwq, dwkv, dwout, dwup1, dwdown1, dwqkv, dwso, dwup2, dwdown2)
        ]
    dwq, dwkv, dwout, dwup1, dwdown1, dwqkv, dwso, dwup2, dwdown2 = sums
    return (
        out[None],
        latent_grad[None],
        token_grad[None],
        dgains[0],
        dgains[1],
        dwq,
        dwkv,
        dwout,
        dgains[2],
        dwup1,
        dwdown1,
        dgains[3],
        dwqkv,
        dwso,
        dgains[4],
        dwup2,
        dwdown2,
    )


def solution(mesh):
    by_row = P("row", "lat", None)
    weight = P("lat", None)
    gain = P("lat")
    parameters = (
        gain, gain, weight, weight, weight, gain, weight, weight, gain, weight, weight, gain,
        weight, weight,
    )
    return jax.shard_map(
        local,
        mesh=mesh,
        in_specs=(by_row, by_row, P("row", "lat"), P("row", "lat"), P("row", None), by_row)
        + parameters,
        out_specs=(by_row, by_row, by_row) + parameters,
        check_vma=False,
    )
```

profile of v0, /device:TPU:0, one launch (start us, length us, event | category | flops | bytes accessed | tf_op | source)
XLA Modules:
  0.0 307.8 jit_solution(3682036306513587571)
XLA Ops:
  0.7 1.3 fusion
  2.0 1.2 broadcast_in_dim.17.scene_ref
  3.2 51.3 %shard_map.323 = (bf16[4,2,4,16,2048]{4,3,2,1,0:T(8,128)(2,1)}, bf16[4,2,4,16,2048]{4,3,2,1,0:T(8,128)(2,1)}, bf16[4,2,4,64,512]{4,3,2,1,0:T(8,128)(2,1)}, bf16[...) custom-call(bf16[4,16,1024]{2,1,0:T(8,128)(2,1)} %bitcast.92, ...), custom_call_target="tpu_custom_call" | custom-call | tf_op jit(solution)/shard_map/pallas_call | solution.py:84
  54.5 19.8 %shard_map.324 = (f32[1024,512]{1,0:T(8,128)}, f32[1024,512]{1,0:T(8,128)}, bf16[1024,512]{1,0:T(8,128)(2,1)}, bf16[1024,512]{1,0:T(8,128)(2,1)}, bf16[1024,512]...) custom-call(bf16[1024,512]{1,0:T(8,128)(2,1)} %bitcast.66, ...), custom_call_target="tpu_custom_call" | custom-call | tf_op jit(solution)/shard_map/pallas_call | solution.py:84
  74.4 43.0 %shard_map.325 = (bf16[1024,512]{1,0:T(8,128)(2,1)}, bf16[8,1024,2048]{2,1,0:T(8,128)(2,1)}, f32[1024,512]{1,0:T(8,128)}, bf16[1024,512]{1,0:T(8,128)(2,1)}, bf1...) custom-call(bf16[1024,512]{1,0:T(8,128)(2,1)} %get-tuple-element.93., ...), custom_call_target="tpu_custom_call" | custom-call | tf_op jit(solution)/shard_map/pallas_call | solution.py:84
  117.4 26.1 %shard_map.326 = (f32[1024,512]{1,0:T(8,128)}, f32[1024,512]{1,0:T(8,128)}, bf16[1024,512]{1,0:T(8,128)(2,1)}, bf16[512,2048]{1,0:T(8,128)(2,1)}, bf16[2048,512]...) custom-call(f32[1024,512]{1,0:T(8,128)} %get-tuple-element.92.x2_ref, ...), custom_call_target="tpu_custom_call" | custom-call | tf_op jit(solution)/shard_map/pallas_call | solution.py:84
  143.5 52.9 %shard_map.327 = (bf16[1024,512]{1,0:T(8,128)(2,1)}, bf16[1024,512]{1,0:T(8,128)(2,1)}, bf16[1024,512]{1,0:T(8,128)(2,1)}, bf16[1024,512]{1,0:T(8,128)(2,1)}, bf...) custom-call(bf16[1024,512]{1,0:T(8,128)(2,1)} %get-tuple-element.93., ...), custom_call_target="tpu_custom_call" | custom-call | tf_op jit(solution)/shard_map/pallas_call | solution.py:84
  196.4 10.1 %shard_map.328 = (f32[1024,512]{1,0:T(8,128)}, bf16[512,1536]{1,0:T(8,128)(2,1)}, f32[8,512]{1,0:T(8,128)}) custom-call(f32[1024,512]{1,0:T(8,128)} %get-tuple-element.92.x2_ref, f32[1024,512]{1,0:T(8,128)} %get-tuple-element.102.g3_ref, bf16[1024,512]{1,0:T(8,128)(2,1)} %get-tuple-element.111.dq_ref, bf16[1024,512]{1,0:T(8,128)(2,1)} %get-tuple-element.112.dk_ref, ...), custom_call_target="tpu_custom_call" | custom-call | tf_op jit(solution)/shard_map/pallas_call | solution.py:84
  206.5 22.9 %shard_map.329 = (f32[1024,512]{1,0:T(8,128)}, bf16[1024,512]{1,0:T(8,128)(2,1)}, bf16[512,2048]{1,0:T(8,128)(2,1)}, bf16[2048,512]{1,0:T(8,128)(2,1)}, bf16[512,512]{1,0:T(8,128)(2,1)}, /*index=5*/f32[8,512]{1,0:T(8,128)}) custom-call(f32[1024,512]{1,0:T(8,128)} %get-tuple-element.101.x1_ref, f32[1024,512]{1,0:T(8,128)} %get-tuple-element.116.g2_ref, ...), custom_call_target="tpu_custom_call" | custom-call | tf_op jit(solution)/shard_map/pallas_call | solution.py:84
  229.4 71.6 %shard_map.330 = (bf16[1024,512]{1,0:T(8,128)(2,1)}, bf16[4,16,1536]{2,1,0:T(8,128)(2,1)}, bf16[4,16,2048]{2,1,0:T(8,128)(2,1)}, bf16[4,64,512]{2,1,0:T(8,128)(2...) custom-call(bf16[1024,512]{1,0:T(8,128)(2,1)} %bitcast.67, ...), custom_call_target="tpu_custom_call" | custom-call | tf_op jit(solution)/shard_map/pallas_call | solution.py:84
  301.0 0.8 constant_dynamic-slice_fusion
  301.7 0.5 slice_bitcast_fusion
  302.2 5.2 %shard_map.331 = (f32[1024,512]{1,0:T(8,128)}, f32[256,512]{1,0:T(8,128)}, f32[64,1024]{1,0:T(8,128)}, f32[64,512]{1,0:T(8,128)}, f32[64,512]{1,0:T(8,128)}, /*i...) custom-call(f32[1024,512]{1,0:T(8,128)} %get-tuple-element.118.base_, ...), custom_call_target="tpu_custom_call" | custom-call | tf_op jit(solution)/shard_map/pallas_call | solution.py:84
where the time goes:
time: 312 us; the launch traced here: 308 us
  Pallas kernels  303 us (97%)
    pallas_call x9, Pallas kernels, call(): pl.pallas_call(kernel, grid=grid, in_specs=in_specs, out_specs=out_specs,...  303 us

commit v1 on v0

--- a/solution.py
+++ b/solution.py
@@ -116,14 +116,17 @@
 
 
 def front_kernel(
-    lat_ref, tok_ref, tags_ref, scene_ref, gain_ref, wq_ref, wkv_ref, wout_ref, wup_ref, wdown_ref, wqkv_ref,
+    lat_rows, lat_ref, tok_ref, tags_ref, scene_ref, gain_ref, wq_ref, wkv_ref, wout_ref, wup_ref, wdown_ref, wqkv_ref,
     x1_ref, x2_ref, q_ref, p_ref, o_ref, kv_ref, q2_ref, k2_ref, v2_ref, win_ref, start_ref,
     bias_ref, sem,
 ):
     @pl.when(pl.program_id(0) == 0)
     def _():
         span, slots = win_ref.shape[0], tok_ref.shape[0]
-        tags, scene = tags_ref[...].astype(F32), scene_ref[0, 0].astype(F32)
+        tags, scenes = tags_ref[...].astype(F32), scene_ref[...]
+        own = lax.axis_index("lat") * lat_rows // LAT_SCENE
+        own = lax.broadcasted_iota(jnp.int32, scenes.shape, 1) == own
+        scene = jnp.sum(jnp.where(own, scenes, 0).astype(F32))
         count = lambda chosen: jnp.sum(jnp.where(chosen, 1.0, 0.0)).astype(jnp.int32)
         before = count((tags >= 0.0) & (tags < scene))
         length = count(tags == scene)
@@ -169,7 +172,7 @@
     block = min(rows, 512)
     r = (block, D)
     return call(
-        front_kernel,
+        functools.partial(front_kernel, rows),
         (rows // block,),
         [
             (latents, r, rows_of),
@@ -332,16 +335,14 @@
     6: (("in_chip", 1),),
     7: (("in_chip", 2),),
     10: (("in_pairs", 0),),
-    15: (("in_pairs", 1),),
+    14: (("in_pairs", 1),),
     16: (("in_pairs", 2),),
-    18: (("in_plane", 0),),
-    20: (("in_plane", 1), ("turn0", 0)),
+    17: (("in_plane", 0),),
+    20: (("in_plane", 1),),
     21: (("in_plane", 2),),
-    22: (("turn1", 0), ("turn0", 1)),
-    24: (("turn2", 0), ("turn1", 1), ("turn0", 2)),
-    26: (("in_line", 0), ("turn2", 1), ("turn1", 2)),
-    28: (("in_line", 1), ("turn2", 2)),
-    30: (("in_line", 2),),
+    23: (("in_line", 0),),
+    27: (("in_line", 1),),
+    29: (("in_line", 2),),
     31: (("end", 0), ("end", 1), ("end", 2)),
 }
 
@@ -1003,7 +1004,7 @@
 
     def copy(self, way, dest):
         index = (way, dest - 1 if way == UP else dest)
-        return send(self.block(dest), self.arrived.at[index], [s for s in self.sems], index, self.here.to_z[way])
+        return send(self.block(dest), self.arrived.at[index], self.sems, index, self.here.to_z[way])
 
     def start(self):
         @pl.when(self.here.z == 0)
@@ -1033,13 +1034,34 @@
             pl.when(self.here.z > dest)(lambda dest=dest: self.copy(DOWN, dest).wait_send())
 
 
+class DirectSum(LineSum):
+    def copy(self, i):
+        return send(self.block(self.here.above[i]), self.arrived.at[0, i], self.sems, (0, i), self.here.line[i])
+
+    def start(self):
+        for i in range(3):
+            self.copy(i).start()
+
+    def turn(self, group):
+        if group == len(LINE) - 1:
+            for i in range(3):
+                self.copy(i).wait()
+            ref, arrived = self.block(self.here.z), self.arrived
+            total = ref[...].astype(F32) + arrived[0, 0].astype(F32)
+            ref[...] = low(total + arrived[0, 1].astype(F32) + arrived[0, 2].astype(F32))
+
+    def finish(self):
+        pass
+
+
 class Staged:
     def __init__(self, rows, cols):
         self.shape = (rows, cols)
 
 
 class WeightSum:
-    def __init__(self, chunks, gains=None, tokens=None):
+    def __init__(self, chunks, gains=None, tokens=None, direct=()):
+        self.direct = direct
         self.chunks, self.inputs, self.scratch, self.staged = [], [], [], []
         self.sources = 0
         for chunk in chunks:
@@ -1148,7 +1170,8 @@
     def line(self, k):
         here, buffers = self.here, self.buffers[k]
         sems = [sem.at[k] for sem in self.z_sems]
-        return LineSum(here, lambda z: buffers[0].at[z, here.y, here.x], buffers[4], sems)
+        kind = DirectSum if k in self.direct else LineSum
+        return kind(here, lambda z: buffers[0].at[z, here.y, here.x], buffers[4], sems)
 
     def finished(self, k):
         for i in range(3):
@@ -1294,8 +1317,8 @@
     kv_sum, dkv_ref, more_ref, kv_sems = scratch[0], scratch[1], scratch[2], scratch[3:5]
     comm.bind(ins, outs, scratch[5:])
     here = comm.here
-    mixed = len(comm.chunks) - 1
-    early = range(mixed)
+    mixed = len(comm.chunks) - 2
+    early, last = range(mixed), mixed + 1
     rows, span = p_ref.shape
     gains = comm.gain_buffers[0]
 
@@ -1333,7 +1356,8 @@
     to_core = send(
         dkv_ref.at[pl.ds(half * (1 - here.c), half)], more_ref, kv_sems, 0, here.to_core)
     to_core.start()
-    comm.stages[1][...] = low(dwq).reshape(comm.stages[1].shape)
+    comm.stages[0][...] = low(dwq).reshape(comm.stages[0].shape)
+    comm.start(mixed)
     gains[2:3], gains[3:4], gains[4:5] = dm1_ref[0:1], ds_ref[0:1], dm2_ref[0:1]
     unit, factor = normed(win_ref[pl.ds(half * here.c, half)].astype(F32))
     gain = gain_ref[1:2, :]
@@ -1344,36 +1368,46 @@
     comm.token_core().start()
     gains[1:2] = dgain
     comm.gain_step(0)
-    comm.stages[0][...] = low(dot_tn(low(unit * gain), dkv)).reshape(comm.stages[0].shape)
-    comm.start(mixed)
+    comm.stages[1][...] = low(dot_tn(low(unit * gain), dkv)).reshape(comm.stages[1].shape)
+    comm.start(last)
     comm.token_place(start_ref[0:1, 0:1])
-    for k in early:
-        comm.in_pairs(k)
     comm.in_chip(mixed)
+    comm.in_pairs(0)
+    comm.in_pairs(1)
     comm.gain_step(1)
+    comm.in_chip(last)
     comm.token_line.turn(0)
-    for k in early:
-        comm.in_plane(k)
+    comm.in_pairs(2)
+    comm.in_plane(0)
     comm.in_pairs(mixed)
-    for k in early:
+    comm.in_plane(1)
+    comm.token_line.turn(1)
+    comm.in_pairs(last)
+    for k in (0, 1):
         comm.turn0(k)
-    comm.token_line.turn(1)
-    for k in early:
+    comm.in_plane(2)
+    comm.gain_step(2)
+    for k in (0, 1):
         comm.turn1(k)
     comm.in_plane(mixed)
-    comm.gain_step(2)
-    for k in early:
+    comm.token_line.turn(2)
+    comm.in_plane(last)
+    for k in (0, 1):
         comm.turn2(k)
-    comm.turn0(mixed)
-    comm.token_line.turn(2)
-    for k in early:
+    for k in (2, mixed):
+        comm.turn0(k)
+    for k in (0, 1):
         comm.in_line(k)
-    comm.turn1(mixed)
+    for k in (2, mixed):
+        comm.turn1(k)
     comm.gain_step(3)
-    comm.turn2(mixed)
+    for k in (2, mixed):
+        comm.turn2(k)
+    comm.in_line(last)
     comm.token_end()
-    comm.in_line(mixed)
-    for k in range(mixed + 1):
+    for k in (2, mixed):
+        comm.in_line(k)
+    for k in range(last + 1):
         comm.end(k)
 
 
@@ -1471,9 +1505,6 @@
     group = LAT_SCENE // rows
     bits = group.bit_length() - 1
 
-    block = place * rows // LAT_SCENE
-    scene = jnp.sum(jnp.where(jnp.arange(scenes) == block, block_scene[0], 0))
-    scene = jnp.broadcast_to(scene, (8, LANES))
     gains = [gain_cross_q, gain_cross_kv, gain_mlp1, gain_self, gain_mlp2]
     first_weights = [[w_cross_kv, w_cross_q, w_cross_out], [w_up1], [w_down1], [w_self_qkv]]
     later_weights = [[w_up2], [w_down2], [w_self_out]]
@@ -1494,7 +1525,7 @@
         )
 
     x1, x2, q, p, o, kv, q2, k2, v2, window, start = front(
-        latents, all_tokens, tags, scene, span, gains, mix, up1, down1, qkv
+        latents, all_tokens, tags, block_scene, span, gains, mix, up1, down1, qkv
     )
     if planes:
         o2, p2, scale2, k2_more, v2_more, *weights = self_forward(q2, (k2,), (v2,), Gather(later_weights))
@@ -1511,7 +1542,7 @@
         keys, values = (k2,), (v2,)
         o2, p2, scale2 = self_forward(q2, keys, values)
     out, g3, do2, dwup2, dwdown2, dwso, dgain_m2 = second(x2, o2, og, gains, so, up2, down2)
-    comm = WeightSum([[dwup2], [dwdown2], [dwso]]) if planes else None
+    comm = WeightSum([[dwup2], [dwdown2], [dwso]], direct=(0, 1, 2)) if planes else None
     dq2, dkv2, early = self_backward(q2, do2, o2, scale2, p2, keys, values, comm)
     if planes:
         dk, dv, dk_more, dv_more = dkv2
@@ -1522,16 +1553,17 @@
     g1, do, dwup1, dwdown1, dwout, dgain_m1 = first_back(x1, g2, o, gains, mix, up1, down1)
     if planes:
         comm = WeightSum(
-            [[dwqkv], [dwup1], [dwdown1], [Staged(D, 2 * D), Staged(D, D), dwout]], gains=(8, D), tokens=slots
+            [[dwqkv], [dwup1], [dwdown1], [Staged(D, D), dwout], [Staged(D, 2 * D)]], gains=(8, D), tokens=slots,
+            direct=(4,),
         )
         term, *late, dgains, token_grad = tail(
             comm, latents, do, p, q, kv, gains, mix, window, start, (dgain_m1, dgain_s, dgain_m2)
         )
         dgains = lax.dynamic_slice_in_dim(dgains, place * (D // 8), D // 8, axis=1)
-        up2, down2, so, qkv, up1, down1, mixed = join([*early, *late])
-        latent_grad, token_grad, dwkv, dwq, dwout, *others = widen(
-            g1, term, [token_grad, mixed, up1, down1, qkv, so, up2, down2],
-            ((D,), (2 * D, D, D), (FF,), (D,), (3 * D,), (D,), (FF,), (D,)),
+        up2, down2, so, qkv, up1, down1, mixed, dwkv = join([*early, *late])
+        latent_grad, token_grad, dwq, dwout, dwkv, *others = widen(
+            g1, term, [token_grad, mixed, dwkv, up1, down1, qkv, so, up2, down2],
+            ((D,), (D, D), (2 * D,), (FF,), (D,), (3 * D,), (D,), (FF,), (D,)),
         )
         sums = dwq, dwkv, dwout, *others
     else:

time: 312 us -> 302 us (0.968)
  Pallas kernels: 303 us -> 296 us
    pallas_call x9, Pallas kernels: 303 us -> 296 us  [call(): pl.pallas_call(kernel, grid=grid, in_specs=in_specs, out_specs=out_specs,...]
where the time goes in v1:
time: 302 us; the launch traced here: 298 us
  Pallas kernels  296 us (98%)
    pallas_call x9, Pallas kernels, call(): pl.pallas_call(kernel, grid=grid, in_specs=in_specs, out_specs=out_specs,...  296 us

profile of v1, /device:TPU:0, one launch (start us, length us, event | category | flops | bytes accessed | tf_op | source)
XLA Modules:
  0.0 298.3 jit_solution(12048525840261973881)
XLA Ops:
  0.7 51.3 %shard_map.323 = (bf16[4,2,4,16,2048]{4,3,2,1,0:T(8,128)(2,1)}, bf16[4,2,4,16,2048]{4,3,2,1,0:T(8,128)(2,1)}, bf16[4,2,4,64,512]{4,3,2,1,0:T(8,128)(2,1)}, bf16[...) custom-call(bf16[4,16,1024]{2,1,0:T(8,128)(2,1)} %bitcast.90, ...), custom_call_target="tpu_custom_call" | custom-call | tf_op jit(solution)/shard_map/pallas_call | solution.py:84
  52.0 20.0 %shard_map.324 = (f32[1024,512]{1,0:T(8,128)}, f32[1024,512]{1,0:T(8,128)}, bf16[1024,512]{1,0:T(8,128)(2,1)}, bf16[1024,512]{1,0:T(8,128)(2,1)}, bf16[1024,512]...) custom-call(bf16[1024,512]{1,0:T(8,128)(2,1)} %bitcast.65, ...), custom_call_target="tpu_custom_call" | custom-call | tf_op jit(solution)/shard_map/pallas_call | solution.py:84
  71.9 42.9 %shard_map.325 = (bf16[1024,512]{1,0:T(8,128)(2,1)}, bf16[8,1024,2048]{2,1,0:T(8,128)(2,1)}, f32[1024,512]{1,0:T(8,128)}, bf16[1024,512]{1,0:T(8,128)(2,1)}, bf1...) custom-call(bf16[1024,512]{1,0:T(8,128)(2,1)} %get-tuple-element.94., ...), custom_call_target="tpu_custom_call" | custom-call | tf_op jit(solution)/shard_map/pallas_call | solution.py:84
  114.9 26.1 %shard_map.326 = (f32[1024,512]{1,0:T(8,128)}, f32[1024,512]{1,0:T(8,128)}, bf16[1024,512]{1,0:T(8,128)(2,1)}, bf16[512,2048]{1,0:T(8,128)(2,1)}, bf16[2048,512]...) custom-call(f32[1024,512]{1,0:T(8,128)} %get-tuple-element.93.x2_ref, ...), custom_call_target="tpu_custom_call" | custom-call | tf_op jit(solution)/shard_map/pallas_call | solution.py:84
  141.0 51.8 %shard_map.327 = (bf16[1024,512]{1,0:T(8,128)(2,1)}, bf16[1024,512]{1,0:T(8,128)(2,1)}, bf16[1024,512]{1,0:T(8,128)(2,1)}, bf16[1024,512]{1,0:T(8,128)(2,1)}, bf...) custom-call(bf16[1024,512]{1,0:T(8,128)(2,1)} %get-tuple-element.94., ...), custom_call_target="tpu_custom_call" | custom-call | tf_op jit(solution)/shard_map/pallas_call | solution.py:84
  192.8 10.1 %shard_map.328 = (f32[1024,512]{1,0:T(8,128)}, bf16[512,1536]{1,0:T(8,128)(2,1)}, f32[8,512]{1,0:T(8,128)}) custom-call(f32[1024,512]{1,0:T(8,128)} %get-tuple-element.93.x2_ref, f32[1024,512]{1,0:T(8,128)} %get-tuple-element.103.g3_ref, bf16[1024,512]{1,0:T(8,128)(2,1)} %get-tuple-element.112.dq_ref, bf16[1024,512]{1,0:T(8,128)(2,1)} %get-tuple-element.113.dk_ref, ...), custom_call_target="tpu_custom_call" | custom-call | tf_op jit(solution)/shard_map/pallas_call | solution.py:84
  202.9 22.9 %shard_map.329 = (f32[1024,512]{1,0:T(8,128)}, bf16[1024,512]{1,0:T(8,128)(2,1)}, bf16[512,2048]{1,0:T(8,128)(2,1)}, bf16[2048,512]{1,0:T(8,128)(2,1)}, bf16[512,512]{1,0:T(8,128)(2,1)}, /*index=5*/f32[8,512]{1,0:T(8,128)}) custom-call(f32[1024,512]{1,0:T(8,128)} %get-tuple-element.102.x1_ref, f32[1024,512]{1,0:T(8,128)} %get-tuple-element.117.g2_ref, ...), custom_call_target="tpu_custom_call" | custom-call | tf_op jit(solution)/shard_map/pallas_call | solution.py:84
  225.8 65.6 %shard_map.330 = (bf16[1024,512]{1,0:T(8,128)(2,1)}, bf16[4,16,1536]{2,1,0:T(8,128)(2,1)}, bf16[4,16,2048]{2,1,0:T(8,128)(2,1)}, bf16[4,64,512]{2,1,0:T(8,128)(2...) custom-call(bf16[1024,512]{1,0:T(8,128)(2,1)} %bitcast.66, ...), custom_call_target="tpu_custom_call" | custom-call | tf_op jit(solution)/shard_map/pallas_call | solution.py:84
  291.4 5.3 %shard_map.331 = (f32[1024,512]{1,0:T(8,128)}, f32[256,512]{1,0:T(8,128)}, f32[64,512]{1,0:T(8,128)}, f32[64,512]{1,0:T(8,128)}, f32[64,1024]{1,0:T(8,128)}, /*i...) custom-call(f32[1024,512]{1,0:T(8,128)} %get-tuple-element.119.base_, ...), custom_call_target="tpu_custom_call" | custom-call | tf_op jit(solution)/shard_map/pallas_call | solution.py:84
  296.7 0.8 constant_dynamic-slice_fusion
  297.5 0.5 slice_bitcast_fusion

commit v2 on v1

--- a/solution.py
+++ b/solution.py
@@ -515,101 +515,105 @@
     )
 
 
-def qkv_back_kernel(
-    x2_ref, g3_ref, dq_ref, dk_ref, dk_more_ref, dv_ref, dv_more_ref, gain_ref, w_ref,
-    g2_ref, dw_ref, dgain_ref,
+def middle_back_kernel(
+    blocks, steps,
+    x2_ref, g3_ref, dq_ref, dk_ref, dk_more_ref, dv_ref, dv_more_ref, x1_ref,
+    o_ref, gain_ref, wqkv_ref, wout_ref, wup_ref, wdown_ref,
+    g1_ref, do_ref, dwqkv_ref, dwup_ref, dwdown_ref, dwout_ref, dgain_s_ref, dgain_m_ref,
+    dw_sum, g2_ref, unit_ref, factor_ref, m_ref, b_ref, dm_ref,
 ):
-    unit, factor = normed(x2_ref[...])
-    gain = gain_ref[3:4, :]
-    bn = low(unit * gain)
-    dq = dq_ref[...]
-    dk = low(dk_ref[...].astype(F32) + dk_more_ref[...].astype(F32))
-    dv = low(dv_ref[...].astype(F32) + dv_more_ref[...].astype(F32))
-    dbn = None
-    for i, part in enumerate((dq, dk, dv)):
-        cols = slice(i * D, (i + 1) * D)
-        dw_ref[:, cols] = low(dot_tn(bn, part))
-        term = dot_nt(part, w_ref[:, cols])
-        dbn = term if dbn is None else dbn + term
-    back, dgain = norm_back(dbn, unit, factor, gain)
-    g2_ref[...] = g3_ref[...] + back
-    dgain_ref[...] = jnp.broadcast_to(dgain, dgain_ref.shape)
-
-
-def qkv_back(x2, g3, dq, dk, dk_more, dv, dv_more, gains, qkv):
-    rows = x2.shape[0]
-    r = (rows, D)
-    return call(
-        qkv_back_kernel,
-        (1,),
-        [(a, r, flat) for a in (x2, g3, dq, dk, dk_more, dv, dv_more)]
-        + [(gains, (8, D), flat), (qkv, (D, 3 * D), flat)],
-        [
-            (r, F32, r, flat),
-            ((D, 3 * D), BF16, (D, 3 * D), flat),
-            ((8, D), F32, (8, D), flat),
-        ],
-    )
-
-
-def first_back_kernel(
-    steps, x1_ref, g2_ref, o_ref, gain_ref, wout_ref, wup_ref, wdown_ref,
-    g1_ref, do_ref, dwup_ref, dwdown_ref, dwout_ref, dgain_ref,
-    m_ref, b_ref, dm_ref,
-):
-    c = pl.program_id(0)
-
-    @pl.when(c == 0)
+    step = pl.program_id(0)
+
+    @pl.when(step == 0)
     def _():
-        unit, _ = normed(x1_ref[...])
-        m_ref[...] = low(unit * gain_ref[2:3, :])
-        b_ref[...] = low(g2_ref[...])
+        dw_sum[...] = jnp.zeros_like(dw_sum)
         dm_ref[...] = jnp.zeros_like(dm_ref)
-
-    m, b = m_ref[...], b_ref[...]
-    h, slope = gelu_both(dot(m, wup_ref[...]))
-    dwdown_ref[...] = low(dot_tn(low(h), b))
-    du = low(slope * dot_nt(b, wdown_ref[...]))
-    dwup_ref[...] = low(dot_tn(m, du))
-    dm_ref[...] += dot_nt(du, wup_ref[...])
-
-    @pl.when(c == steps - 1)
+        dgain_s_ref[...] = jnp.zeros_like(dgain_s_ref)
+
+    @pl.when(step < blocks)
     def _():
+        count = x2_ref.shape[0]
+        at = pl.ds(pl.multiple_of(step * count, count), count)
+        unit, factor = normed(x2_ref[...])
+        gain = gain_ref[3:4, :]
+        bn = low(unit * gain)
+        dk = low(dk_ref[...].astype(F32) + dk_more_ref[...].astype(F32))
+        dv = low(dv_ref[...].astype(F32) + dv_more_ref[...].astype(F32))
+        dbn = None
+        for i, part in enumerate((dq_ref[...], dk, dv)):
+            cols = slice(i * D, (i + 1) * D)
+            dw_sum[:, cols] += dot_tn(bn, part)
+            term = dot_nt(part, wqkv_ref[:, cols])
+            dbn = term if dbn is None else dbn + term
+        back, dgain = norm_back(dbn, unit, factor, gain)
+        g2 = g3_ref[...] + back
+        g2_ref[at] = g2
+        b_ref[at] = low(g2)
+        dgain_s_ref[...] += jnp.broadcast_to(dgain, dgain_s_ref.shape)
         unit, factor = normed(x1_ref[...])
-        back, dgain = norm_back(dm_ref[...], unit, factor, gain_ref[2:3, :])
+        unit_ref[at] = unit
+        factor_ref[at] = jnp.broadcast_to(factor, (count, LANES))
+        m_ref[at] = low(unit * gain_ref[2:3, :])
+
+    @pl.when(step >= blocks)
+    def _():
+        m, b = m_ref[...], b_ref[...]
+        h, slope = gelu_both(dot(m, wup_ref[...]))
+        dwdown_ref[...] = low(dot_tn(low(h), b))
+        du = low(slope * dot_nt(b, wdown_ref[...]))
+        dwup_ref[...] = low(dot_tn(m, du))
+        dm_ref[...] += dot_nt(du, wup_ref[...])
+
+    @pl.when(step == blocks + steps - 1)
+    def _():
+        dwqkv_ref[...] = low(dw_sum[...])
+        back, dgain = norm_back(dm_ref[...], unit_ref[...], factor_ref[:, 0:1], gain_ref[2:3, :])
         g1 = g2_ref[...] + back
         g1_ref[...] = g1
-        dgain_ref[...] = jnp.broadcast_to(dgain, dgain_ref.shape)
+        dgain_m_ref[...] = jnp.broadcast_to(dgain, dgain_m_ref.shape)
         b1 = low(g1)
         dwout_ref[...] = low(dot_tn(o_ref[...], b1))
         do_ref[...] = low(dot_nt(b1, wout_ref[...]))
 
 
-def first_back(x1, g2, o, gains, mix, up1, down1):
+def middle_back(x2, g3, dq, dk, dk_more, dv, dv_more, x1, o, gains, qkv, mix, up1, down1):
     rows = x1.shape[0]
-    steps = FF // FF_STEP
+    block = min(rows, 512)
+    blocks, steps = rows // block, FF // FF_STEP
     r = (rows, D)
+    row_block = lambda s: (jnp.minimum(s, blocks - 1), 0)
+    part = lambda s: jnp.maximum(s - blocks, 0)
     return call(
-        functools.partial(first_back_kernel, steps),
-        (steps,),
-        [
-            (x1, r, flat),
-            (g2, r, flat),
+        functools.partial(middle_back_kernel, blocks, steps),
+        (blocks + steps,),
+        [(a, (block, D), row_block) for a in (x2, g3, dq, dk, dk_more, dv, dv_more, x1)]
+        + [
             (o, r, flat),
             (gains, (8, D), flat),
+            (qkv, (D, 3 * D), flat),
             (mix, (D, D), column(3)),
-            (up1, (D, FF_STEP), lambda c: (0, c)),
-            (down1, (FF_STEP, D), lambda c: (c, 0)),
+            (up1, (D, FF_STEP), lambda s: (0, part(s))),
+            (down1, (FF_STEP, D), lambda s: (part(s), 0)),
         ],
         [
             (r, F32, r, flat),
             (r, BF16, r, flat),
-            ((D, FF), BF16, (D, FF_STEP), lambda c: (0, c)),
-            ((FF, D), BF16, (FF_STEP, D), lambda c: (c, 0)),
+            ((D, 3 * D), BF16, (D, 3 * D), flat),
+            ((D, FF), BF16, (D, FF_STEP), lambda s: (0, part(s))),
+            ((FF, D), BF16, (FF_STEP, D), lambda s: (part(s), 0)),
             ((D, D), BF16, (D, D), flat),
             ((8, D), F32, (8, D), flat),
+            ((8, D), F32, (8, D), flat),
         ],
-        [pltpu.VMEM(r, BF16), pltpu.VMEM(r, BF16), pltpu.VMEM(r, F32)],
+        [
+            pltpu.VMEM((D, 3 * D), F32),
+            pltpu.VMEM(r, F32),
+            pltpu.VMEM(r, F32),
+            pltpu.VMEM((rows, LANES), F32),
+            pltpu.VMEM(r, BF16),
+            pltpu.VMEM(r, BF16),
+            pltpu.VMEM(r, F32),
+        ],
     )
 
 
@@ -1549,8 +1553,9 @@
     else:
         dk, dk_more = halve(dkv2[0], place, bits)
         dv, dv_more = halve(dkv2[1], place, bits)
-    g2, dwqkv, dgain_s = qkv_back(x2, g3, dq2, dk, dk_more, dv, dv_more, gains, qkv)
-    g1, do, dwup1, dwdown1, dwout, dgain_m1 = first_back(x1, g2, o, gains, mix, up1, down1)
+    g1, do, dwqkv, dwup1, dwdown1, dwout, dgain_s, dgain_m1 = middle_back(
+        x2, g3, dq2, dk, dk_more, dv, dv_more, x1, o, gains, qkv, mix, up1, down1
+    )
     if planes:
         comm = WeightSum(
             [[dwqkv], [dwup1], [dwdown1], [Staged(D, D), dwout], [Staged(D, 2 * D)]], gains=(8, D), tokens=slots,

time: 302 us -> 299 us (0.990)
    pallas_call x9 -> x8, Pallas kernels: 296 us -> 293 us  [call(): pl.pallas_call(kernel, grid=grid, in_specs=in_specs, out_specs=out_specs,...]
where the time goes in v2:
time: 299 us; the launch traced here: 295 us
  Pallas kernels  293 us (98%)
    pallas_call x8, Pallas kernels, call(): pl.pallas_call(kernel, grid=grid, in_specs=in_specs, out_specs=out_specs,...  293 us

profile of v2, /device:TPU:0, one launch (start us, length us, event | category | flops | bytes accessed | tf_op | source)
XLA Modules:
  0.0 295.4 jit_solution(10509130248842235835)
XLA Ops:
  0.7 51.3 %shard_map.323 = (bf16[4,2,4,16,2048]{4,3,2,1,0:T(8,128)(2,1)}, bf16[4,2,4,16,2048]{4,3,2,1,0:T(8,128)(2,1)}, bf16[4,2,4,64,512]{4,3,2,1,0:T(8,128)(2,1)}, bf16[...) custom-call(bf16[4,16,1024]{2,1,0:T(8,128)(2,1)} %bitcast.90, ...), custom_call_target="tpu_custom_call" | custom-call | tf_op jit(solution)/shard_map/pallas_call | solution.py:84
  52.0 20.0 %shard_map.324 = (f32[1024,512]{1,0:T(8,128)}, f32[1024,512]{1,0:T(8,128)}, bf16[1024,512]{1,0:T(8,128)(2,1)}, bf16[1024,512]{1,0:T(8,128)(2,1)}, bf16[1024,512]...) custom-call(bf16[1024,512]{1,0:T(8,128)(2,1)} %bitcast.65, ...), custom_call_target="tpu_custom_call" | custom-call | tf_op jit(solution)/shard_map/pallas_call | solution.py:84
  72.0 43.0 %shard_map.325 = (bf16[1024,512]{1,0:T(8,128)(2,1)}, bf16[8,1024,2048]{2,1,0:T(8,128)(2,1)}, f32[1024,512]{1,0:T(8,128)}, bf16[1024,512]{1,0:T(8,128)(2,1)}, bf1...) custom-call(bf16[1024,512]{1,0:T(8,128)(2,1)} %get-tuple-element.93., ...), custom_call_target="tpu_custom_call" | custom-call | tf_op jit(solution)/shard_map/pallas_call | solution.py:84
  114.9 26.1 %shard_map.326 = (f32[1024,512]{1,0:T(8,128)}, f32[1024,512]{1,0:T(8,128)}, bf16[1024,512]{1,0:T(8,128)(2,1)}, bf16[512,2048]{1,0:T(8,128)(2,1)}, bf16[2048,512]...) custom-call(f32[1024,512]{1,0:T(8,128)} %get-tuple-element.92.x2_ref, ...), custom_call_target="tpu_custom_call" | custom-call | tf_op jit(solution)/shard_map/pallas_call | solution.py:84
  141.0 51.4 %shard_map.327 = (bf16[1024,512]{1,0:T(8,128)(2,1)}, bf16[1024,512]{1,0:T(8,128)(2,1)}, bf16[1024,512]{1,0:T(8,128)(2,1)}, bf16[1024,512]{1,0:T(8,128)(2,1)}, bf...) custom-call(bf16[1024,512]{1,0:T(8,128)(2,1)} %get-tuple-element.93., ...), custom_call_target="tpu_custom_call" | custom-call | tf_op jit(solution)/shard_map/pallas_call | solution.py:84
  192.5 30.4 %shard_map.328 = (f32[1024,512]{1,0:T(8,128)}, bf16[1024,512]{1,0:T(8,128)(2,1)}, bf16[512,1536]{1,0:T(8,128)(2,1)}, bf16[512,2048]{1,0:T(8,128)(2,1)}, bf16[204...) custom-call(f32[1024,512]{1,0:T(8,128)} %get-tuple-element.92.x2_ref, ...), custom_call_target="tpu_custom_call" | custom-call | tf_op jit(solution)/shard_map/pallas_call | solution.py:84
  222.8 65.7 %shard_map.329 = (bf16[1024,512]{1,0:T(8,128)(2,1)}, bf16[4,16,1536]{2,1,0:T(8,128)(2,1)}, bf16[4,16,2048]{2,1,0:T(8,128)(2,1)}, bf16[4,64,512]{2,1,0:T(8,128)(2...) custom-call(bf16[1024,512]{1,0:T(8,128)(2,1)} %bitcast.66, ...), custom_call_target="tpu_custom_call" | custom-call | tf_op jit(solution)/shard_map/pallas_call | solution.py:84
  288.6 5.3 %shard_map.330 = (f32[1024,512]{1,0:T(8,128)}, f32[256,512]{1,0:T(8,128)}, f32[64,512]{1,0:T(8,128)}, f32[64,512]{1,0:T(8,128)}, f32[64,1024]{1,0:T(8,128)}, /*i...) custom-call(f32[1024,512]{1,0:T(8,128)} %get-tuple-element.117.base_, ...), custom_call_target="tpu_custom_call" | custom-call | tf_op jit(solution)/shard_map/pallas_call | solution.py:84
  293.9 0.8 constant_dynamic-slice_fusion
  294.6 0.5 slice_bitcast_fusion

commit v3 on v2

--- a/solution.py
+++ b/solution.py
@@ -749,7 +749,7 @@
 
 
 TOKEN_PARTS = 4
-AHEAD = 2
+AHEAD = 3
 GAP = 2
 SHIFT = 3
 WEIGHT, TOKENS, NOTES = range(3)

time: 299 us -> 299 us (level)
  no operation moved by 1% of the time
where the time goes in v3:
time: 299 us; the launch traced here: 295 us
  Pallas kernels  293 us (98%)
    pallas_call x8, Pallas kernels, call(): pl.pallas_call(kernel, grid=grid, in_specs=in_specs, out_specs=out_specs,...  293 us

profile of v3, /device:TPU:0, one launch (start us, length us, event | category | flops | bytes accessed | tf_op | source)
XLA Modules:
  0.0 295.3 jit_solution(162132982551484003)
XLA Ops:
  0.7 51.0 %shard_map.323 = (bf16[4,2,4,16,2048]{4,3,2,1,0:T(8,128)(2,1)}, bf16[4,2,4,16,2048]{4,3,2,1,0:T(8,128)(2,1)}, bf16[4,2,4,64,512]{4,3,2,1,0:T(8,128)(2,1)}, bf16[...) custom-call(bf16[4,16,1024]{2,1,0:T(8,128)(2,1)} %bitcast.90, ...), custom_call_target="tpu_custom_call" | custom-call | tf_op jit(solution)/shard_map/pallas_call | solution.py:84
  51.7 19.9 %shard_map.324 = (f32[1024,512]{1,0:T(8,128)}, f32[1024,512]{1,0:T(8,128)}, bf16[1024,512]{1,0:T(8,128)(2,1)}, bf16[1024,512]{1,0:T(8,128)(2,1)}, bf16[1024,512]...) custom-call(bf16[1024,512]{1,0:T(8,128)(2,1)} %bitcast.65, ...), custom_call_target="tpu_custom_call" | custom-call | tf_op jit(solution)/shard_map/pallas_call | solution.py:84
  71.6 43.0 %shard_map.325 = (bf16[1024,512]{1,0:T(8,128)(2,1)}, bf16[8,1024,2048]{2,1,0:T(8,128)(2,1)}, f32[1024,512]{1,0:T(8,128)}, bf16[1024,512]{1,0:T(8,128)(2,1)}, bf1...) custom-call(bf16[1024,512]{1,0:T(8,128)(2,1)} %get-tuple-element.93., ...), custom_call_target="tpu_custom_call" | custom-call | tf_op jit(solution)/shard_map/pallas_call | solution.py:84
  114.6 26.1 %shard_map.326 = (f32[1024,512]{1,0:T(8,128)}, f32[1024,512]{1,0:T(8,128)}, bf16[1024,512]{1,0:T(8,128)(2,1)}, bf16[512,2048]{1,0:T(8,128)(2,1)}, bf16[2048,512]...) custom-call(f32[1024,512]{1,0:T(8,128)} %get-tuple-element.92.x2_ref, ...), custom_call_target="tpu_custom_call" | custom-call | tf_op jit(solution)/shard_map/pallas_call | solution.py:84
  140.7 51.5 %shard_map.327 = (bf16[1024,512]{1,0:T(8,128)(2,1)}, bf16[1024,512]{1,0:T(8,128)(2,1)}, bf16[1024,512]{1,0:T(8,128)(2,1)}, bf16[1024,512]{1,0:T(8,128)(2,1)}, bf...) custom-call(bf16[1024,512]{1,0:T(8,128)(2,1)} %get-tuple-element.93., ...), custom_call_target="tpu_custom_call" | custom-call | tf_op jit(solution)/shard_map/pallas_call | solution.py:84
  192.3 30.4 %shard_map.328 = (f32[1024,512]{1,0:T(8,128)}, bf16[1024,512]{1,0:T(8,128)(2,1)}, bf16[512,1536]{1,0:T(8,128)(2,1)}, bf16[512,2048]{1,0:T(8,128)(2,1)}, bf16[204...) custom-call(f32[1024,512]{1,0:T(8,128)} %get-tuple-element.92.x2_ref, ...), custom_call_target="tpu_custom_call" | custom-call | tf_op jit(solution)/shard_map/pallas_call | solution.py:84
  222.6 65.8 %shard_map.329 = (bf16[1024,512]{1,0:T(8,128)(2,1)}, bf16[4,16,1536]{2,1,0:T(8,128)(2,1)}, bf16[4,16,2048]{2,1,0:T(8,128)(2,1)}, bf16[4,64,512]{2,1,0:T(8,128)(2...) custom-call(bf16[1024,512]{1,0:T(8,128)(2,1)} %bitcast.66, ...), custom_call_target="tpu_custom_call" | custom-call | tf_op jit(solution)/shard_map/pallas_call | solution.py:84
  288.5 5.3 %shard_map.330 = (f32[1024,512]{1,0:T(8,128)}, f32[256,512]{1,0:T(8,128)}, f32[64,512]{1,0:T(8,128)}, f32[64,512]{1,0:T(8,128)}, f32[64,1024]{1,0:T(8,128)}, /*i...) custom-call(f32[1024,512]{1,0:T(8,128)} %get-tuple-element.117.base_, ...), custom_call_target="tpu_custom_call" | custom-call | tf_op jit(solution)/shard_map/pallas_call | solution.py:84
  293.8 0.8 constant_dynamic-slice_fusion
  294.5 0.5 slice_bitcast_fusion
